TPU v7x, 32 devices: a whole 2x2x4 slice. The times are simulated.
32 devices in a mesh: gx: 8 (over z, x), gy: 4 (over y, core).
Axes of the slice: x: 2, y: 2, z: 4, core: 2. Of those that a mesh axis runs over, the one named last changes fastest.
Arguments:
- hydro: float32 [192, 192, 792], P('gx', 'gy'), may hold values from 0.05 to 2
- winds: float32 [192, 192, 24], P('gx', 'gy'), may hold values from -0.3 to 0.3
- cloud_mask: int32 [192, 192], P('gx', 'gy'), may hold values from 0 to 1, as said below
- coal_kernel: bfloat16 [4356, 66], replicated, may hold values from -0.09375 to 0.09375
- block_mask: int32 [6, 6], replicated, may hold values 0 or 1
Outputs:
- hydro_next: float32 [192, 192, 792], P('gx', 'gy')
Inputs may be any that keep to these rules, and one draw needn't show every extreme that they name: `cloud_mask`: exactly 4608 columns are cloudy; the columns of one aligned tile of 24 x 48 are all cloudy.
All inputs are finite; a program needn't handle non-finite values.
Results may differ from a plain program's by a relative error of at most 0.0017.
Values may be sent and summed in bfloat16 or wider, within the bound.
A program may use at most 128 MiB of HBM per device.

v0:
```python
import jax
import jax.numpy as jnp
from jax import lax
from jax.sharding import PartitionSpec as P

BLK = 11


def padded_2(array, sides, width):
    for axis, dim in sides:
        count, length = (lax.axis_size(axis), array.shape[dim])
        up = [(i, (i + 1) % count) for i in range(count)]
        down = [(j, i) for i, j in up]
        last = lax.slice_in_dim(array, length - width, length, axis=dim)
        initial = lax.slice_in_dim(array, 0, width, axis=dim)
        before = lax.ppermute(last, axis, up)
        after = lax.ppermute(initial, axis, down)
        array = jnp.concatenate([before, array, after], axis=dim)
    return array


def coalesce(rows2d, chan, kernel_wide):
    total = rows2d.shape[0] * (rows2d.shape[1] // chan)
    cells = rows2d.reshape(total, chan)
    pieces = 1
    while total % pieces != 0 or total // pieces > 2048:
        pieces = pieces + 1

    def one_block(block):
        wide = block.astype(jnp.float32)
        pairs = (wide[:, :, None] * wide[:, None, :]).astype(jnp.bfloat16).reshape(-1, chan * chan)
        return jnp.dot(pairs, kernel_wide, preferred_element_type=jnp.float32).astype(jnp.bfloat16)

    result = lax.map(one_block, cells.reshape(pieces, total // pieces, chan))
    result = result.reshape(total, kernel_wide.shape[1])[:, :chan]
    return result.reshape(rows2d.shape[0], rows2d.shape[1])


def per_device(hydro, winds, cloud_mask, coal_kernel, block_mask):
    size_x, size_y, width = hydro.shape
    levels = winds.shape[2] // 2
    chan = width // levels
    stacked = jnp.concatenate([hydro, winds], axis=2)
    padded = padded_2(stacked, (("gx", 0), ("gy", 1)), 1)
    field = padded[:, :, :width]
    wind_x = padded[:, :, width : width + levels]
    wind_y = padded[:, :, width + levels :]
    along_x = field[:, 1:-1]
    face_x = jnp.repeat(0.5 * (wind_x[:-1, 1:-1] + wind_x[1:, 1:-1]), chan, axis=2)
    flux_x = jnp.maximum(face_x, 0.0) * along_x[:-1] + jnp.minimum(face_x, 0.0) * along_x[1:]
    along_y = field[1:-1]
    face_y = jnp.repeat(0.5 * (wind_y[1:-1, :-1] + wind_y[1:-1, 1:]), chan, axis=2)
    flux_y = jnp.maximum(face_y, 0.0) * along_y[:, :-1] + jnp.minimum(face_y, 0.0) * along_y[:, 1:]
    q_adv = field[1:-1, 1:-1] - (flux_x[1:] - flux_x[:-1]) - (flux_y[:, 1:] - flux_y[:, :-1])
    blocks_count = block_mask.shape[0]
    onehot = ((jnp.arange(chan) // BLK)[:, None] == jnp.arange(blocks_count)[None, :]).astype(
        jnp.float32
    )
    blockmap = jnp.dot(jnp.dot(onehot, block_mask.astype(jnp.float32)), onehot.T)
    kernel_eff = jnp.where(
        blockmap.reshape(chan * chan, 1) > 0.5, coal_kernel, jnp.zeros_like(coal_kernel)
    )
    lanes = (chan + 127) // 128 * 128
    kernel_wide = jnp.concatenate(
        [kernel_eff, jnp.zeros((chan * chan, lanes - chan), jnp.bfloat16)], axis=1
    )
    ncols = size_x * size_y
    flat = cloud_mask.reshape(-1)
    columns = q_adv.astype(jnp.bfloat16).reshape(ncols, width)
    size_gx = lax.axis_size("gx")
    size_gy = lax.axis_size("gy")
    devices = size_gx * size_gy
    me_index = lax.axis_index("gx") * size_gy + lax.axis_index("gy")
    count = jnp.sum(flat)
    counts = lax.all_gather(count.reshape(1), ("gx", "gy"), axis=0, tiled=True)
    starts = jnp.cumsum(counts) - counts
    ends = starts + counts
    offset = starts[me_index]
    send_rows = ncols // devices
    owned = ncols // 8
    source_index = jnp.nonzero(flat, size=ncols, fill_value=0)[0].astype(jnp.int32)
    slot_pos = jnp.arange(send_rows, dtype=jnp.int32)[:, None]
    slot_dev = jnp.arange(devices, dtype=jnp.int32)[None, :]
    send_rank = (slot_pos * devices + (slot_dev - offset) % devices).reshape(-1)
    send_alive = send_rank < count
    outgoing = jnp.where(
        send_alive[:, None], columns[source_index[send_rank]], jnp.zeros((), jnp.bfloat16)
    )
    outgoing = outgoing.reshape(send_rows, devices, width)
    position = jnp.arange(send_rows)[:, None]
    rel_rank = position * devices + ((me_index - starts) % devices)[None, :]
    alive_slot = rel_rank < counts[None, :]
    slot_of = jnp.where(alive_slot, (starts[None, :] + rel_rank) // devices, owned)
    global_rank = jnp.arange(owned) * devices + me_index
    source_dev = jnp.sum((ends[None, :] <= global_rank[:, None]).astype(jnp.int32), axis=1)
    local_rank = global_rank - starts[source_dev]
    arrive_row = local_rank // devices * devices + source_dev
    arrived = lax.all_to_all(outgoing, ("gx", "gy"), split_axis=1, concat_axis=1, tiled=True)
    gathered = arrived.reshape(send_rows * devices, width)[arrive_row]
    computed = coalesce(gathered, chan, kernel_wide)
    extended = jnp.concatenate([computed, jnp.zeros((1, width), jnp.bfloat16)], axis=0)
    returned = lax.all_to_all(
        extended[slot_of.reshape(-1)].reshape(send_rows, devices, width),
        ("gx", "gy"),
        split_axis=1,
        concat_axis=1,
        tiled=True,
    )
    returned = returned.reshape(send_rows * devices, width)
    column_rank = jnp.maximum(jnp.cumsum(flat) - 1, 0)
    back_row = column_rank // devices * devices + (column_rank % devices + offset) % devices
    tendency = jnp.where(flat[:, None] > 0, returned[back_row].astype(jnp.float32), 0.0)
    result = q_adv + tendency.reshape(size_x, size_y, width)
    return result


def solution(mesh):
    in_specs = (P("gx", "gy", None), P("gx", "gy", None), P("gx", "gy"), P(), P())
    out_specs = P("gx", "gy", None)
    return jax.shard_map(
        per_device, mesh=mesh, in_specs=in_specs, out_specs=out_specs, check_vma=False
    )
```

profile of v0, /device:TPU:0, one launch (start us, length us, event | category | flops | bytes accessed | tf_op | source)
XLA Modules:
  0.0 341.7 jit_solution(962298888700188795)
XLA Ops:
  0.0 1.2 copy.91
  1.2 1.1 pad_maximum_fusion.15
  2.3 6.0 %collective-permute-start.1 = (f32[1,48,816]{2,1,0:T(8,128)S(1)}, f32[1,48,816]{2,1,0:T(8,128)S(1)}, u32[]{:S(2)}, u32[]{:S(2)}) collective-permute-start(f32[1,48,816]{2,1,0:T(8,128)S(1)} %get-tuple-element.30), channel_id=1, source_target_pairs={{4,0},{8,4},{12,8},{16,12},{20,16},{24,20},{28,24},{0,28},{5,1},{9... | collective-permute-start | bytes 470024 | tf_op jit(solution)/shard_map/ppermute | solution.py:17
  8.4 0.7 fusion.35
  9.1 0.8 dynamic-update-slice
  9.9 40.1 %all-reduce.2 = s32[32]{0:T(128)S(1)} all-reduce(s32[32]{0:T(128)S(1)} %dynamic-update-slice), channel_id=1, replica_groups=mesh['gx'=8,'gy'=4] {'gx','gy'}, use_global_device_ids=true, to_apply=%add.2 | all-reduce | flops 32 | bytes 256
  50.3 0.7 dynamic_slice.6
  50.9 0.7 and_select_fusion.6
  51.7 0.7 add_compare_fusion
  53.0 9.2 %scatter_custom_fusion = s32[1152]{0:T(1024)S(1)} fusion(s32[1152]{0:T(1024)S(1)} %fusion.21, s32[1152]{0:T(1024)S(1)} %broadcast.571, s32[]{:T(128)} %constant.140.clone.1), kind=kCustom, calls=%fused_computation.112 | custom fusion | flops 1152 | bytes 4612 | tf_op jit(solution)/shard_map/scatter-add | solution.py:81
  62.8 0.8 fusion.17
  63.7 6.5 %gather_fusion = s32[1152]{0:T(1024)S(1)} fusion(s32[1152]{0:T(1024)S(1)} %fusion.17, s32[2048]{0:T(1024)S(1)} %pad_clamp_fusion.3), kind=kCustom, calls=%fused_computation | custom fusion | bytes 13824 | tf_op jit(solution)/shard_map/gather | solution.py:87
  70.3 1.6 pad_maximum_fusion.19
  72.0 0.5 collective-permute-start.2
  72.8 0.4 broadcast_maximum_fusion
  73.2 5.7 %broadcast_in_dim.87 = f32[25,48,12,66]{3,2,1,0:T(8,128)} broadcast(f32[25,48,12]{2,1,0:T(8,128)S(1)} %broadcast_minimum_fusion), dimensions={0,1,2} | broadcast | bytes 3859200 | tf_op jit(solution)/shard_map/broadcast_in_dim | solution.py:49
  78.9 9.2 %min.15 = f32[25,48,792]{2,1,0:T(8,128)} reshape(f32[25,48,12,66]{3,2,1,0:T(8,128)} %broadcast_in_dim.87) | data formatting | bytes 7603200 | tf_op jit(solution)/shard_map/min | solution.py:50
  88.1 5.7 %broadcast_in_dim.86 = f32[25,48,12,66]{3,2,1,0:T(8,128)} broadcast(f32[25,48,12]{2,1,0:T(8,128)S(1)} %get-tuple-element.23), dimensions={0,1,2} | broadcast | bytes 3859200 | tf_op jit(solution)/shard_map/broadcast_in_dim | solution.py:49
  93.8 9.2 %max.26 = f32[25,48,792]{2,1,0:T(8,128)} reshape(f32[25,48,12,66]{3,2,1,0:T(8,128)} %broadcast_in_dim.86) | data formatting | bytes 7603200 | tf_op jit(solution)/shard_map/max | solution.py:50
  103.0 8.9 %fusion.4 = f32[25,48,792]{2,1,0:T(8,128)} fusion(f32[25,48,792]{2,1,0:T(8,128)} %min.15, f32[1,48,816]{2,1,0:T(8,128)S(1)} %collective-permute-done.1, f32[24,48,24]{2,1,0:T(8,128)S(1)} %copy.91, f32[24,48,792]{2,1,0:T(8,128)} %param.5, f32[25,48,792]{2,1,0:T(8,128)} %max.26, f32[1,48,816]{2,1,0:T(8,128)S(1)} %collective-permute-done), kind=kLoop, calls=%fused_computation.21 | loop fusion | flops 6652800 | bytes 15478272 | tf_op jit(solution)/shard_map/add | solution.py:50
  111.9 0.8 pad_maximum_fusion.12
  113.7 5.6 %broadcast_in_dim.89 = f32[24,49,12,66]{3,2,0,1:T(8,128)} broadcast(f32[24,49,12]{2,0,1:T(8,128)S(1)} %copy.96), dimensions={0,1,2} | broadcast | bytes 3782016 | tf_op jit(solution)/shard_map/broadcast_in_dim | solution.py:52
  119.3 9.1 %min.17 = f32[24,49,792]{2,0,1:T(8,128)} reshape(f32[24,49,12,66]{3,2,0,1:T(8,128)} %broadcast_in_dim.89) | data formatting | bytes 7451136 | tf_op jit(solution)/shard_map/min | solution.py:53
  128.7 5.6 %broadcast_in_dim.88 = f32[24,49,12,66]{3,2,0,1:T(8,128)} broadcast(f32[24,49,12]{2,0,1:T(8,128)S(1)} %copy.94), dimensions={0,1,2} | broadcast | bytes 3782016 | tf_op jit(solution)/shard_map/broadcast_in_dim | solution.py:52
  134.3 9.1 %max.28 = f32[24,49,792]{2,0,1:T(8,128)} reshape(f32[24,49,12,66]{3,2,0,1:T(8,128)} %broadcast_in_dim.88) | data formatting | bytes 7451136 | tf_op jit(solution)/shard_map/max | solution.py:53
  143.4 8.6 %fusion.1 = f32[24,49,792]{2,1,0:T(8,128)S(1)} fusion(f32[26,1,816]{2,1,0:T(1,128)S(1)} %collective-permute-done.3, f32[1,48,816]{2,1,0:T(8,128)S(1)} %collective-permute-done.1, f32[1,48,816]{2,1,0:T(8,128)S(1)} %collective-permute-done, f32[24,48,24]{2,1,0:T(8,128)S(1)} %copy.91, f32[24,48,792]{2,1,0:T(8,128)} %param.5, ...), kind=kLoop, calls=%fused_computation.10 | loop fusion | flops 10245312 | bytes 15419904 | tf_op jit(solution)/shard_map/add | solution.py:53
  152.0 5.4 %fusion.36 = (bf16[24,48,792]{2,1,0:T(8,128)(2,1)S(1)}, f32[24,48,792]{2,1,0:T(8,128)}) fusion(f32[24,49,792]{2,1,0:T(8,128)S(1)} %fusion.1, f32[24,48,792]{2,1,0:T(8,128)S(1)} %copy-done.2, f32[25,48,792]{2,1,0:T(8,128)} %fusion.4), kind=kLoop, calls=%fused_computation.134 | loop fusion | flops 4561920 | bytes 23721984 | tf_op jit(solution)/shard_map/convert_element_type | solution.py:69
  157.4 4.9 %gather_fusion.1 = bf16[1152,792]{1,0:T(8,128)(2,1)} fusion(bf16[1152,792]{1,0:T(8,128)(2,1)S(1)} %bitcast.67, s32[2048]{0:T(1024)S(1)} %pad_clamp_fusion.2), kind=kCustom, calls=%fused_computation.1 | custom fusion | bytes 3654144 | tf_op jit(solution)/shard_map/gather | solution.py:87
  162.3 3.9 %copy_select_fusion = bf16[36,32,792]{2,0,1:T(8,128)(2,1)} fusion(bf16[36,32,792]{2,1,0:T(8,128)(2,1)} %bitcast.70, pred[36,32]{0,1:T(8,128)(4,1)S(1)} %copy.99), kind=kLoop, calls=%fused_computation.32 | loop fusion | flops 912384 | bytes 3650688 | tf_op jit(solution)/shard_map/jit(_where)/select_n | solution.py:86
  166.2 5.9 %all-to-all-start = ((bf16[36,32,792]{2,0,1:T(8,128)(2,1)}), bf16[36,32,792]{2,0,1:T(8,128)(2,1)S(1)}, u32[]{:S(2)}, u32[]{:S(2)}) async-start(bf16[36,32,792]{2,0,1:T(8,128)(2,1)} %copy_select_fusion), calls=%async_computation | async-start | bytes 4587520 | tf_op jit(solution)/shard_map/all_to_all | solution.py:98
  172.2 1.6 gather_fusion.2
  173.8 0.4 convolution_compare_fusion
  174.6 0.9 broadcast_select_fusion
  175.6 49.4 %all-to-all-done = bf16[36,32,792]{2,0,1:T(8,128)(2,1)S(1)} async-done(((bf16[36,32,792]{2,0,1:T(8,128)(2,1)}), bf16[36,32,792]{2,0,1:T(8,128)(2,1)S(1)}, u32[]{:S(2)}, u32[]{:S(2)}) %all-to-all-start) | async-done | bytes 1824800 | tf_op jit(solution)/shard_map/all_to_all | solution.py:98
  224.9 1.6 copy.101
  226.5 2.9 gather_fusion.3
  229.5 0.4 reshape.600
  230.2 6.1 %multiply_convert_fusion = bf16[1728,66,66]{0,2,1:T(8,128)(2,1)} fusion(f32[1728,66]{0,1:T(8,128)S(1)} %copy.102), kind=kLoop, calls=%fused_computation.7 | loop fusion | flops 15054336 | bytes 15510528 | tf_op jit(solution)/shard_map/while/body/eval_jaxpr/convert_element_type | solution.py:31
  236.3 20.8 %convert_element_type.60 = bf16[1728,4356]{0,1:T(8,128)(2,1)} reshape(bf16[1728,66,66]{0,2,1:T(8,128)(2,1)} %multiply_convert_fusion) | data formatting | bytes 30108672 | tf_op jit(solution)/shard_map/while/body/eval_jaxpr/convert_element_type | solution.py:31
  257.1 7.7 %fusion.9 = bf16[1728,128]{0,1:T(8,128)(2,1)S(1)} fusion(bf16[1728,4356]{0,1:T(8,128)(2,1)} %convert_element_type.60, bf16[4356,66]{0,1:T(8,128)(2,1)S(1)} %copy-done.4), kind=kOutput, calls=%fused_computation.33 | convolution fusion | flops 1926955008 | bytes 16071696 | tf_op jit(solution)/shard_map/while/body/eval_jaxpr/dot_general | solution.py:32
  265.5 4.7 %gather_fusion.4 = bf16[1152,792]{1,0:T(8,128)(2,1)S(1)} fusion(bf16[145,792]{1,0:T(8,128)(2,1)S(1)} %concatenate.36, s32[2048]{0:T(1024)S(1)} %pad_clamp_fusion.1), kind=kCustom, calls=%fused_computation.4 | custom fusion | bytes 3654144 | tf_op jit(solution)/shard_map/gather | solution.py:103
  270.2 2.0 copy.105
  272.3 4.3 %all-to-all-start.1 = ((bf16[36,32,792]{2,0,1:T(8,128)(2,1)}), bf16[36,32,792]{2,0,1:T(8,128)(2,1)}, u32[]{:S(2)}, u32[]{:S(2)}) async-start(bf16[36,32,792]{2,0,1:T(8,128)(2,1)} %copy.105), calls=%async_computation.1 | async-start | bytes 4587520 | tf_op jit(solution)/shard_map/all_to_all | solution.py:102
  277.2 0.7 fusion.25
  278.0 51.6 %all-to-all-done.1 = bf16[36,32,792]{2,0,1:T(8,128)(2,1)} async-done(((bf16[36,32,792]{2,0,1:T(8,128)(2,1)}), bf16[36,32,792]{2,0,1:T(8,128)(2,1)}, u32[]{:S(2)}, u32[]{:S(2)}) %all-to-all-start.1) | async-done | bytes 1824800 | tf_op jit(solution)/shard_map/all_to_all | solution.py:102
  329.6 1.9 copy.106
  331.5 4.9 %gather_fusion.5 = bf16[1152,792]{1,0:T(8,128)(2,1)} fusion(bf16[1152,792]{1,0:T(8,128)(2,1)S(1)} %bitcast.68, s32[2048]{0:T(1024)S(1)} %pad_clamp_fusion), kind=kCustom, calls=%fused_computation.5 | custom fusion | bytes 3654144 | tf_op jit(solution)/shard_map/gather | solution.py:112
  336.4 5.3 %fusion.8 = f32[24,48,792]{2,1,0:T(8,128)} fusion(f32[24,48,792]{2,1,0:T(8,128)} %get-tuple-element.22, bf16[24,48,792]{2,1,0:T(8,128)(2,1)} %bitcast.72, pred[24,48]{1,0:T(8,128)(4,1)S(1)} %broadcast_compare_fusion.1), kind=kLoop, calls=%fused_computation.31 | loop fusion | flops 2737152 | bytes 9124992 | tf_op jit(solution)/shard_map/add | solution.py:113
  (77 shorter events, 5.7 us)
Async XLA Ops:
  0.0 8.3 %copy-start.5 = (s32[24,48]{1,0:T(8,128)S(1)}, s32[24,48]{1,0:T(8,128)}, u32[]{:S(2)}) copy-start(s32[24,48]{1,0:T(8,128)} %param.7) | copy-start | bytes 13828
  2.3 68.0 %collective-permute-start.1 = (f32[1,48,816]{2,1,0:T(8,128)S(1)}, f32[1,48,816]{2,1,0:T(8,128)S(1)}, u32[]{:S(2)}, u32[]{:S(2)}) collective-permute-start(f32[1,48,816]{2,1,0:T(8,128)S(1)} %get-tuple-element.30), channel_id=1, source_target_pairs={{4,0},{8,4},{12,8},{16,12},{20,16},{24,20},{28,24},{0,28},{5,1},{9... | collective-permute-start | bytes 470024 | tf_op jit(solution)/shard_map/ppermute | solution.py:17
  8.3 61.9 %collective-permute-start = (f32[1,48,816]{2,1,0:T(8,128)S(1)}, f32[1,48,816]{2,1,0:T(8,128)S(1)}, u32[]{:S(2)}, u32[]{:S(2)}) collective-permute-start(f32[1,48,816]{2,1,0:T(8,128)S(1)} %get-tuple-element.29), channel_id=1, source_target_pairs={{0,4},{4,8},{8,12},{12,16},{16,20},{20,24},{24,28},{28,0},{1,5},{5... | collective-permute-start | bytes 470024 | tf_op jit(solution)/shard_map/ppermute | solution.py:16
  70.2 2.6 copy-start
  71.9 40.0 %collective-permute-start.3 = (f32[26,1,816]{2,1,0:T(1,128)S(1)}, f32[26,1,816]{2,1,0:T(1,128)S(1)}, u32[]{:S(2)}, u32[]{:S(2)}) collective-permute-start(f32[26,1,816]{2,1,0:T(1,128)S(1)} %get-tuple-element.28), channel_id=1, source_target_pairs={{1,0},{2,1},{3,2},{0,3},{5,4},{6,5},{7,6},{4,7},{9,8},{10,9},{11,1... | collective-permute-start | bytes 254600 | tf_op jit(solution)/shard_map/ppermute | solution.py:17
  72.0 39.9 %collective-permute-start.2 = (f32[26,1,816]{2,1,0:T(1,128)S(1)}, f32[26,1,816]{2,1,0:T(1,128)S(1)}, u32[]{:S(2)}, u32[]{:S(2)}) collective-permute-start(f32[26,1,816]{2,1,0:T(1,128)S(1)} %get-tuple-element.27), channel_id=1, source_target_pairs={{0,1},{1,2},{2,3},{3,0},{4,5},{5,6},{6,7},{7,4},{8,9},{9,10},{10,1... | collective-permute-start | bytes 254600 | tf_op jit(solution)/shard_map/ppermute | solution.py:16
  103.0 8.9 %copy-start.1 = (f32[24,48,792]{2,1,0:T(8,128)S(1)}, f32[24,48,792]{2,1,0:T(8,128)}, u32[]{:S(2)}) copy-start(f32[24,48,792]{2,1,0:T(8,128)} %param.5) | copy-start | bytes 10948612
  143.4 8.6 %copy-start.2 = (f32[24,48,792]{2,1,0:T(8,128)S(1)}, f32[24,48,792]{2,1,0:T(8,128)}, u32[]{:S(2)}) copy-start(f32[24,48,792]{2,1,0:T(8,128)} %param.5) | copy-start | bytes 10948612
  162.3 11.5 %copy-start.6 = (s32[6,6]{1,0:T(8,128)S(1)}, s32[6,6]{1,0:T(8,128)}, u32[]{:S(2)}) copy-start(s32[6,6]{1,0:T(8,128)} %param.9) | copy-start | bytes 436
  162.3 12.3 %copy-start.3 = (bf16[4356,66]{0,1:T(8,128)(2,1)S(1)}, bf16[4356,66]{0,1:T(8,128)(2,1)}, u32[]{:S(2)}) copy-start(bf16[4356,66]{0,1:T(8,128)(2,1)} %param.8) | copy-start | bytes 1724980
  166.2 58.7 %all-to-all-start = ((bf16[36,32,792]{2,0,1:T(8,128)(2,1)}), bf16[36,32,792]{2,0,1:T(8,128)(2,1)S(1)}, u32[]{:S(2)}, u32[]{:S(2)}) async-start(bf16[36,32,792]{2,0,1:T(8,128)(2,1)} %copy_select_fusion), calls=%async_computation | async-start | bytes 4587520 | tf_op jit(solution)/shard_map/all_to_all | solution.py:98
  236.3 20.8 %copy-start.4 = (bf16[4356,66]{0,1:T(8,128)(2,1)S(1)}, bf16[4356,66]{0,1:T(8,128)(2,1)}, u32[]{:S(2)}) copy-start(bf16[4356,66]{0,1:T(8,128)(2,1)} %broadcast_select_fusion) | copy-start | bytes 1724980
  272.3 57.3 %all-to-all-start.1 = ((bf16[36,32,792]{2,0,1:T(8,128)(2,1)}), bf16[36,32,792]{2,0,1:T(8,128)(2,1)}, u32[]{:S(2)}, u32[]{:S(2)}) async-start(bf16[36,32,792]{2,0,1:T(8,128)(2,1)} %copy.105), calls=%async_computation.1 | async-start | bytes 4587520 | tf_op jit(solution)/shard_map/all_to_all | solution.py:102
where the time goes:
time: 343 us; the launch traced here: 342 us
  local copies, waits for them, and re-layouts  118 us (34%)
  waiting for transfers between devices  101 us (29%)
  other arithmetic  57.7 us (17%)
  blocking collectives  40.1 us (12%)
  starting transfers between devices  16.7 us (5%)
  matrix products  8.16 us (2%)
    all_to_all x1, waiting for transfers between devices, per_device(): lax.all_to_all(extended[slot_of.reshape(-1)].reshape(send_rows, devices,...  51.6 us
    all_to_all x1, waiting for transfers between devices, per_device(): lax.all_to_all(outgoing, ('gx', 'gy'), split_axis=1, concat_axis=1, tiled...  49.4 us
    unnamed x1, blocking collectives  40.1 us
    convert_element_type x1, local copies, waits for them, and re-layouts, one_block(): (wide[:, :, None] * wide[:, None, :]).astype(jnp.bfloat16)  20.8 us
    broadcast_in_dim x2, local copies, waits for them, and re-layouts, per_device(): jnp.repeat(0.5 * (wind_x[:-1, 1:-1] + wind_x[1:, 1:-1]), chan, axis=2)  11.3 us
    broadcast_in_dim x2, local copies, waits for them, and re-layouts, per_device(): jnp.repeat(0.5 * (wind_y[1:-1, :-1] + wind_y[1:-1, 1:]), chan, axis=2)  11.2 us
    max x2, local copies, waits for them, and re-layouts, per_device(): jnp.maximum(face_y, 0.0) * along_y[:, :-1]  9.41 us
    min x2, local copies, waits for them, and re-layouts, per_device(): jnp.minimum(face_y, 0.0) * along_y[:, 1:]  9.41 us
  transfers between devices with their start and end apart: 6, of which 2 were waited for; matrix products, arithmetic and copies ran while one was open for 19% of the time, Pallas kernels for 0%

commit v1 on v0

v1 whole, which is shorter than its diff:
```python
import jax
import jax.numpy as jnp
from jax import lax
from jax.experimental import pallas as pl
from jax.experimental.pallas import tpu as pltpu
from jax.sharding import PartitionSpec as P

BLK = 11
ROWS = 16
LANES = 128
DEPTH = 256


def round_up(value, unit):
    return (value + unit - 1) // unit * unit


def edges(array, axis, dim):
    count, length = lax.axis_size(axis), array.shape[dim]
    up = [(i, (i + 1) % count) for i in range(count)]
    down = [(j, i) for i, j in up]
    last = lax.index_in_dim(array, length - 1, dim, keepdims=False)
    first = lax.index_in_dim(array, 0, dim, keepdims=False)
    return last, first, up, down


def folded_kernel(coal_kernel, block_mask, chan):
    of_bin = jnp.repeat(jnp.repeat(block_mask, BLK, axis=0), BLK, axis=1)
    cube = coal_kernel.astype(jnp.float32).T.reshape(chan, chan, chan)
    cube = jnp.where(of_bin[None] > 0, cube, 0.0)
    both = cube + cube.transpose(0, 2, 1)
    whole = chan // ROWS * ROWS
    at = jnp.arange(chan)
    same = (at[:, None] // ROWS == at[None, :] // ROWS)[None]
    used = jnp.where(same, cube, both).astype(jnp.bfloat16)
    parts = []
    for first in range(0, whole, ROWS):
        piece = used[:, first : first + ROWS, first:whole]
        parts.append(piece.reshape(chan, -1))
    if whole < chan:
        parts.append(used[:, whole:, :whole].reshape(chan, -1))
        corner = jnp.pad(used[:, whole:, whole:], ((0, 0), (0, 0), (0, ROWS - (chan - whole))))
        parts.append(corner.reshape(chan, -1))
    flat = jnp.concatenate(parts, axis=1)
    return jnp.pad(flat, ((0, round_up(chan, ROWS) - chan), (0, round_up(flat.shape[1], DEPTH) - flat.shape[1])))


def pair_blocks(chan):
    whole = chan // ROWS * ROWS
    runs = [(i, j) for i in range(whole) for j in range(i // ROWS * ROWS, whole, ROWS)]
    runs += [(i, j) for i in range(whole, chan) for j in range(0, whole, ROWS)]
    runs += [(i, whole) for i in range(whole, chan)]
    return runs


def three_parts(value):
    high = value.astype(jnp.bfloat16)
    rest = value - high.astype(jnp.float32)
    middle = rest.astype(jnp.bfloat16)
    low = (rest - middle.astype(jnp.float32)).astype(jnp.bfloat16)
    return jnp.concatenate([high, middle, low], axis=1)


def step_kernel(levels, chan, q_ref, w_ref, left_ref, right_ref, below_ref, above_ref, mask_ref, spread_ref, fold_ref,
                out_ref, turned_ref, back_ref, flux_ref, tall_ref, wtall_ref):
    size_x, size_y, width = q_ref.shape
    top = 8

    def spread(face):
        return jnp.dot(three_parts(face), spread_ref[...], preferred_element_type=jnp.float32)

    def upwind(face, before, after):
        return jnp.maximum(face, 0.0) * before + jnp.minimum(face, 0.0) * after

    u_first = w_ref[0][:, :levels]
    face = spread(0.5 * (left_ref[:, width : width + levels] + u_first))
    flux_ref[...] = upwind(face, left_ref[:, :width], q_ref[0])

    def advect(x, q_next, u_next):
        here = q_ref[x]
        winds = w_ref[x]
        tall_ref[top : top + size_y] = here
        tall_ref[top - 1 : top] = below_ref[x][:, :width]
        tall_ref[top + size_y : top + size_y + 1] = above_ref[x][:, :width]
        wtall_ref[top : top + size_y] = winds
        wtall_ref[top - 1 : top] = below_ref[x][:, width:]
        wtall_ref[top + size_y : top + size_y + 1] = above_ref[x][:, width:]
        v = winds[:, levels:]
        v_before = wtall_ref[top - 1 : top - 1 + size_y][:, levels:]
        v_after = wtall_ref[top + 1 : top + 1 + size_y][:, levels:]
        faces = jnp.concatenate(
            [0.5 * (winds[:, :levels] + u_next), 0.5 * (v_before + v), 0.5 * (v + v_after)], axis=0
        )
        wide = spread(faces)
        flux_next = upwind(wide[:size_y], here, q_next)
        g_here = upwind(wide[size_y : 2 * size_y], tall_ref[top - 1 : top - 1 + size_y], here)
        g_next = upwind(wide[2 * size_y :], here, tall_ref[top + 1 : top + 1 + size_y])
        result = here - (flux_next - flux_ref[...]) - (g_next - g_here)
        flux_ref[...] = flux_next
        out_ref[pl.ds(pl.multiple_of(x * size_y, 8), size_y), :] = result

    def advect_inner(x, carry):
        advect(x, q_ref[x + 1], w_ref[x + 1][:, :levels])
        return carry

    lax.fori_loop(0, size_x - 1, advect_inner, 0)
    advect(size_x - 1, right_ref[:, :width], right_ref[:, width : width + levels])

    runs = pair_blocks(chan)
    per_chunk = DEPTH // ROWS
    nothing = jnp.zeros((ROWS, LANES), jnp.bfloat16)
    long = turned_ref.shape[0]

    def collide(block, carry):
        rows = pl.ds(pl.multiple_of(block * LANES, LANES), LANES)
        advected = out_ref[rows, :]
        turned_ref[...] = jnp.concatenate(
            [advected, jnp.zeros((LANES, long - width), jnp.float32)], axis=1
        ).T
        cloudy = mask_ref[block] > 0
        for level in range(0, levels, 2):
            starts = (level * chan, (level + 1) * chan)
            tiles = [
                [turned_ref[s + j : s + j + ROWS].astype(jnp.bfloat16) for j in range(0, chan, ROWS)]
                for s in starts
            ]
            total = jnp.zeros((fold_ref.shape[0], 2 * LANES), jnp.float32)
            for chunk in range(0, len(runs), per_chunk):
                halves = []
                for s, tile in zip(starts, tiles):
                    made = []
                    for i, j in runs[chunk : chunk + per_chunk]:
                        one = jnp.broadcast_to(turned_ref[s + i : s + i + 1], (ROWS, LANES)).astype(jnp.bfloat16)
                        made.append(one * tile[j // ROWS])
                    made += [nothing] * (per_chunk - len(made))
                    halves.append(jnp.concatenate(made, axis=0))
                pairs = jnp.concatenate(halves, axis=1)
                columns = slice(chunk * ROWS, chunk * ROWS + DEPTH)
                total += jnp.dot(fold_ref[:, columns], pairs, preferred_element_type=jnp.float32)
            rounded = total.astype(jnp.bfloat16).astype(jnp.float32)
            for half, s in enumerate(starts):
                kept = rounded[:chan, half * LANES : (half + 1) * LANES]
                back_ref[s : s + chan] = jnp.where(cloudy, kept, 0.0)
        out_ref[rows, :] = advected + back_ref[...].T[:, :width]
        return carry

    back_ref[...] = jnp.zeros_like(back_ref)
    lax.fori_loop(0, size_x * size_y // LANES, collide, 0)


def per_device(hydro, winds, cloud_mask, coal_kernel, block_mask):
    size_x, size_y, width = hydro.shape
    levels = winds.shape[2] // 2
    chan = width // levels
    sides = []
    for axis, dim in (("gx", 0), ("gy", 1)):
        shape = (size_y, -1) if dim == 0 else (size_x, 1, -1)
        last, first, up, down = edges(hydro, axis, dim)
        wlast, wfirst, _, _ = edges(winds, axis, dim)
        sides.append(lax.ppermute(jnp.concatenate([last, wlast], axis=1), axis, up).reshape(shape))
        sides.append(lax.ppermute(jnp.concatenate([first, wfirst], axis=1), axis, down).reshape(shape))
    fold = folded_kernel(coal_kernel, block_mask, chan)
    onto = (jnp.arange(levels)[:, None] == jnp.arange(width)[None, :] // chan).astype(jnp.bfloat16)
    onto = jnp.concatenate([onto] * 3, axis=0)
    mask = cloud_mask.reshape(-1, 1, LANES)
    long = round_up(width, LANES)
    result = pl.pallas_call(
        lambda *refs: step_kernel(levels, chan, *refs),
        out_shape=jax.ShapeDtypeStruct((size_x * size_y, width), jnp.float32),
        in_specs=[pl.BlockSpec(memory_space=pltpu.VMEM)] * 9,
        out_specs=pl.BlockSpec(memory_space=pltpu.VMEM),
        scratch_shapes=[
            pltpu.VMEM((long, LANES), jnp.float32),
            pltpu.VMEM((long, LANES), jnp.float32),
            pltpu.VMEM((size_y, width), jnp.float32),
            pltpu.VMEM((size_y + 16, width), jnp.float32),
            pltpu.VMEM((size_y + 16, 2 * levels), jnp.float32),
        ],
        compiler_params=pltpu.CompilerParams(vmem_limit_bytes=40 * 2**20),
    )(hydro, winds, *sides, mask, onto, fold)
    return result.reshape(size_x, size_y, width)


def solution(mesh):
    in_specs = (P("gx", "gy", None), P("gx", "gy", None), P("gx", "gy"), P(), P())
    out_specs = P("gx", "gy", None)
    return jax.shard_map(
        per_device, mesh=mesh, in_specs=in_specs, out_specs=out_specs, check_vma=False
    )
```

time: 343 us -> 63.2 us (0.18)
  waiting for transfers between devices: 101 us -> 0.01 us
  local copies, waits for them, and re-layouts: 118 us -> 18 us
  other arithmetic: 57.7 us -> 7.7 us
  blocking collectives: 40.1 us -> 0 us
  Pallas kernels: 0 us -> 29.1 us
  starting transfers between devices: 16.7 us -> 7.74 us
  matrix products: 8.16 us -> 0 us
    all_to_all x2 -> x0, waiting for transfers between devices: 101 us -> none  [the longest x1 51.6 us: per_device(): lax.all_to_all(extended[slot_of.reshape(-1)].reshape(send_rows, devices,...]
    unnamed x1 -> x0, blocking collectives: 40.1 us -> none
    pallas_call x0 -> x1, Pallas kernels: none -> 29.1 us  [per_device(): pl.pallas_call(lambda *refs: step_kernel(levels, chan, *refs), out_shape=...]
    gather x6 -> x0, local copies, waits for them, and re-layouts: 25.5 us -> none  [the longest x1 6.47 us: per_device(): source_index[send_rank]]
    add x5 -> x0, other arithmetic: 22.9 us -> none  [the longest x1 8.89 us: per_device(): jnp.maximum(face_x, 0.0) * along_x[:-1]]
    broadcast_in_dim x4 -> x2, local copies, waits for them, and re-layouts: 22.6 us -> 0.09 us  [folded_kernel(): of_bin = jnp.repeat(jnp.repeat(block_mask, BLK, axis=0), BLK, axis=1)]
    convert_element_type x3 -> x0, local copies, waits for them, and re-layouts: 21.5 us -> none  [the longest x1 20.8 us: one_block(): (wide[:, :, None] * wide[:, None, :]).astype(jnp.bfloat16)]
    max x3 -> x0, local copies, waits for them, and re-layouts: 18.6 us -> none  [the longest x2 9.41 us: per_device(): jnp.maximum(face_y, 0.0) * along_y[:, :-1]]
  transfers between devices with their start and end apart: 6 -> 4, of which waited for: 2 -> 0; matrix products, arithmetic and copies ran while one was open for 19% -> 34% of each run, Pallas kernels for 0% -> 0%
where the time goes in v1:
time: 63.2 us; the launch traced here: 62.8 us
  Pallas kernels  29.1 us (46%)
  local copies, waits for them, and re-layouts  18 us (28%)
  starting transfers between devices  7.74 us (12%)
  other arithmetic  7.7 us (12%)
    pallas_call x1, Pallas kernels, per_device(): pl.pallas_call(lambda *refs: step_kernel(levels, chan, *refs), out_shape=...  29.1 us
    ppermute x2, starting transfers between devices, per_device(): lax.ppermute(jnp.concatenate([first, wfirst], axis=1), axis, down)  4.8 us
    unnamed x23, local copies, waits for them, and re-layouts  4.03 us
    select_n x1, local copies, waits for them, and re-layouts, folded_kernel(): cube = jnp.where(of_bin[None] > 0, cube, 0.0)  3.27 us
    ppermute x2, starting transfers between devices, per_device(): lax.ppermute(jnp.concatenate([last, wlast], axis=1), axis, up)  2.94 us
    reshape x1, local copies, waits for them, and re-layouts, folded_kernel(): cube = coal_kernel.astype(jnp.float32).T.reshape(chan, chan, chan)  2.22 us
    convert_element_type x1, other arithmetic, folded_kernel(): used = jnp.where(same, cube, both).astype(jnp.bfloat16)  2.02 us
    gt x4, local copies, waits for them, and re-layouts, folded_kernel(): cube = jnp.where(of_bin[None] > 0, cube, 0.0)  1.63 us
  transfers between devices with their start and end apart: 4, of which 0 were waited for; matrix products, arithmetic and copies ran while one was open for 34% of the time, Pallas kernels for 0%

profile of v1, /device:TPU:0, one launch (start us, length us, event | category | flops | bytes accessed | tf_op | source)
XLA Modules:
  0.0 62.8 jit_solution(8078375218293647837)
XLA Ops:
  0.0 1.3 %copy.48.refs_1_ = f32[24,48,24]{2,1,0:T(8,128)S(1)} copy(f32[24,48,24]{1,2,0:T(8,128)} %param.6) | data formatting | bytes 221184 | tf_op args[1]
  1.3 1.0 %slice_bitcast_fusion = (f32[48,792]{1,0:T(8,128)S(1)}, f32[48,792]{1,0:T(8,128)S(1)}) fusion(f32[24,48,792]{2,1,0:T(8,128)} %refs_0_.1), kind=kLoop, calls=%fused_computation.6 | loop fusion | bytes 608256 | tf_op jit(solution)/shard_map/squeeze | solution.py:23
  2.3 0.1 pad_maximum_fusion
  2.4 2.9 %collective-permute-start = (f32[48,816]{1,0:T(8,128)S(1)}, f32[48,816]{1,0:T(8,128)S(1)}, u32[]{:S(2)}, u32[]{:S(2)}) collective-permute-start(f32[48,816]{1,0:T(8,128)S(1)} %pad_maximum_fusion), channel_id=1, source_target_pairs={{0,4},{4,8},{8,12},{12,16},{16,20},{20,24},{24,28},{28,0},{1,5},{5... | collective-permute-start | bytes 470024 | tf_op jit(solution)/shard_map/ppermute | solution.py:160
  5.3 0.7 %pad_maximum_fusion.1 = f32[48,816]{1,0:T(8,128)} fusion(f32[48,24]{1,0:T(8,128)S(1)} %get-tuple-element.9, f32[48,792]{1,0:T(8,128)S(1)} %get-tuple-element.7), kind=kLoop, calls=%fused_computation.5 | loop fusion | flops 39168 | bytes 313344 | tf_op jit(solution)/shard_map/concatenate | solution.py:161
  6.1 3.1 %collective-permute-start.1 = (f32[48,816]{1,0:T(8,128)}, f32[48,816]{1,0:T(8,128)S(1)}, u32[]{:S(2)}, u32[]{:S(2)}) collective-permute-start(f32[48,816]{1,0:T(8,128)} %pad_maximum_fusion.1), channel_id=1, source_target_pairs={{4,0},{8,4},{12,8},{16,12},{20,16},{24,20},{28,24},{0,28},{5,1},{9... | collective-permute-start | bytes 470024 | tf_op jit(solution)/shard_map/ppermute | solution.py:161
  9.1 0.1 fusion.5
  9.3 1.4 %fusion.4 = (f32[24,1,792]{2,1,0:T(1,128)S(1)}, f32[24,1,792]{2,1,0:T(1,128)S(1)}) fusion(f32[24,48,792]{2,1,0:T(8,128)} %refs_0_.1), kind=kLoop, calls=%fused_computation.35 | loop fusion | bytes 304128 | tf_op jit(solution)/shard_map/slice | solution.py:23
  10.7 0.2 copy.50
  10.9 0.7 %pad_maximum_fusion.2 = f32[24,816]{1,0:T(8,128)} fusion(f32[24,24]{1,0:T(8,128)S(1)} %bitcast.33, f32[24,792]{1,0:T(8,128)S(1)} %bitcast.29), kind=kLoop, calls=%fused_computation.9 | loop fusion | flops 19584 | bytes 156672 | tf_op jit(solution)/shard_map/concatenate | solution.py:160
  11.6 0.0 collective-permute-start.2
  11.7 0.2 copy.52
  11.9 0.7 %pad_maximum_fusion.3 = f32[24,816]{1,0:T(8,128)} fusion(f32[24,24]{1,0:T(8,128)S(1)} %bitcast.32, f32[24,792]{1,0:T(8,128)S(1)} %bitcast.30), kind=kLoop, calls=%fused_computation.10 | loop fusion | flops 19584 | bytes 156672 | tf_op jit(solution)/shard_map/concatenate | solution.py:161
  12.6 1.7 %collective-permute-start.3 = (f32[24,816]{1,0:T(8,128)}, f32[24,816]{1,0:T(8,128)}, u32[]{:S(2)}, u32[]{:S(2)}) collective-permute-start(f32[24,816]{1,0:T(8,128)} %pad_maximum_fusion.3), channel_id=1, source_target_pairs={{1,0},{2,1},{3,2},{0,3},{5,4},{6,5},{7,6},{4,7},{9,8},{10,9},{11,1... | collective-permute-start | bytes 235016 | tf_op jit(solution)/shard_map/ppermute | solution.py:161
  14.3 0.6 and_select_fusion
  14.9 1.1 %convert_bitcast_fusion = f32[66,4356]{1,0:T(8,128)} fusion(bf16[4356,66]{0,1:T(8,128)(2,1)S(1)} %copy-done.2), kind=kLoop, calls=%fused_computation.2 | loop fusion | flops 287496 | bytes 1724976 | tf_op jit(solution)/shard_map/reshape | solution.py:29
  16.0 2.2 %reshape.185 = f32[66,66,66]{2,1,0:T(8,128)S(1)} reshape(f32[66,4356]{1,0:T(8,128)} %convert_bitcast_fusion) | data formatting | bytes 2299968 | tf_op jit(solution)/shard_map/reshape | solution.py:29
  18.3 0.1 copy.39
  18.4 0.1 broadcast_in_dim.32
  18.5 0.1 gt.21
  18.6 0.6 gt.22
  19.2 0.8 %copy.40 = pred[66,66]{1,0:T(8,128)(4,1)S(1)} copy(pred[66,66]{0,1:T(8,128)(4,1)} %gt.22) | data formatting | bytes 8712 | tf_op jit(solution)/shard_map/gt | solution.py:30
  20.0 1.6 %broadcast_select_fusion = f32[66,66,66]{2,1,0:T(8,128)} fusion(f32[66,66,66]{2,1,0:T(8,128)S(1)} %reshape.185, pred[66,66]{1,0:T(8,128)(4,1)S(1)} %copy.40), kind=kLoop, calls=%fused_computation.3 | loop fusion | flops 287496 | bytes 2304324 | tf_op jit(solution)/shard_map/jit(_where)/select_n | solution.py:30
  21.6 3.3 %copy.41 = f32[66,66,66]{1,2,0:T(8,128)} copy(f32[66,66,66]{2,1,0:T(8,128)} %broadcast_select_fusion) | data formatting | bytes 2299968 | tf_op jit(solution)/shard_map/jit(_where)/select_n | solution.py:30
  24.9 0.1 broadcast_compare_fusion
  25.0 2.0 %fusion = bf16[66,66,66]{2,1,0:T(8,128)(2,1)S(1)} fusion(f32[66,66,66]{1,2,0:T(8,128)} %copy.41, pred[66,66]{1,0:T(8,128)(4,1)S(1)} %broadcast_compare_fusion, f32[66,66,66]{2,1,0:T(8,128)S(1)} %reshape.185, pred[66,66]{1,0:T(8,128)(4,1)S(1)} %copy.40), kind=kLoop, calls=%fused_computation.1 | loop fusion | flops 1149984 | bytes 2883672 | tf_op jit(solution)/shard_map/convert_element_type | solution.py:35
  27.0 0.1 slice.59
  27.2 0.0 copy-start.3
  27.2 0.1 slice.60
  27.3 0.1 slice.61
  27.5 0.1 slice.63
  27.6 0.2 reshape.177
  27.9 0.3 reshape.178
  28.1 0.3 copy.42
  28.5 0.1 copy.45
  28.6 0.3 copy.43
  28.9 0.1 copy.46
  29.0 0.1 reshape.181
  29.1 0.1 copy.53
  29.2 0.1 copy.47
  29.5 0.1 reshape.174.refs_6_
  29.6 0.0 collective-permute-done.2
  29.6 0.9 %reshape.172.refs_4_ = f32[24,1,816]{2,1,0:T(1,128)S(1)} reshape(f32[24,816]{1,0:T(8,128)} %collective-permute-done.2) | data formatting | bytes 156672 | tf_op jit(solution)/shard_map/reshape | solution.py:160
  30.6 0.9 %reshape.173.refs_5_ = f32[24,1,816]{2,1,0:T(1,128)S(1)} reshape(f32[24,816]{1,0:T(8,128)} %collective-permute-done.3) | data formatting | bytes 156672 | tf_op jit(solution)/shard_map/reshape | solution.py:161
  31.6 0.0 collective-permute-done.refs_2_
  31.6 0.0 copy-start
  31.6 2.2 %copy-done = f32[24,48,792]{2,1,0:T(8,128)S(1)} copy-done((f32[24,48,792]{2,1,0:T(8,128)S(1)}, f32[24,48,792]{2,1,0:T(8,128)}, u32[]{:S(2)}) %copy-start) | copy-done | bytes 3649560
  33.8 29.1 %shard_map.55 = f32[1152,792]{1,0:T(8,128)} custom-call(f32[24,48,792]{2,1,0:T(8,128)S(1)} %copy-done, f32[24,48,24]{2,1,0:T(8,128)S(1)} %copy.48.refs_1_, f32[48,816]{1,0:T(8,128)S(1)} %collective-permute-done.refs_2_, f32[48,816]{1,0:T(8,128)S(1)} %collective-permute-done.1.refs_3_, f32[24,1,816]{2,1,0:T(1,128)S(1)} %reshape.172.refs_4_, ...), custom_call_target="tpu_custom_call" | custom-call | tf_op jit(solution)/shard_map/pallas_call | solution.py:167
  (29 shorter events, 0.3 us)
Async XLA Ops:
  0.0 9.1 %copy-start.1 = (f32[24,48,24]{1,2,0:T(8,128)S(1)}, f32[24,48,24]{1,2,0:T(8,128)}, u32[]{:S(2)}) copy-start(f32[24,48,24]{1,2,0:T(8,128)} %param.6) | copy-start | bytes 331780
  0.0 14.9 %copy-start.2 = (bf16[4356,66]{0,1:T(8,128)(2,1)S(1)}, bf16[4356,66]{0,1:T(8,128)(2,1)}, u32[]{:S(2)}) copy-start(bf16[4356,66]{0,1:T(8,128)(2,1)} %param.8) | copy-start | bytes 1724980
  2.4 29.2 %collective-permute-start = (f32[48,816]{1,0:T(8,128)S(1)}, f32[48,816]{1,0:T(8,128)S(1)}, u32[]{:S(2)}, u32[]{:S(2)}) collective-permute-start(f32[48,816]{1,0:T(8,128)S(1)} %pad_maximum_fusion), channel_id=1, source_target_pairs={{0,4},{4,8},{8,12},{12,16},{16,20},{20,24},{24,28},{28,0},{1,5},{5... | collective-permute-start | bytes 470024 | tf_op jit(solution)/shard_map/ppermute | solution.py:160
  6.1 25.5 %collective-permute-start.1 = (f32[48,816]{1,0:T(8,128)}, f32[48,816]{1,0:T(8,128)S(1)}, u32[]{:S(2)}, u32[]{:S(2)}) collective-permute-start(f32[48,816]{1,0:T(8,128)} %pad_maximum_fusion.1), channel_id=1, source_target_pairs={{4,0},{8,4},{12,8},{16,12},{20,16},{24,20},{28,24},{0,28},{5,1},{9... | collective-permute-start | bytes 470024 | tf_op jit(solution)/shard_map/ppermute | solution.py:161
  11.6 18.0 %collective-permute-start.2 = (f32[24,816]{1,0:T(8,128)}, f32[24,816]{1,0:T(8,128)}, u32[]{:S(2)}, u32[]{:S(2)}) collective-permute-start(f32[24,816]{1,0:T(8,128)} %pad_maximum_fusion.2), channel_id=1, source_target_pairs={{0,1},{1,2},{2,3},{3,0},{4,5},{5,6},{6,7},{7,4},{8,9},{9,10},{10,1... | collective-permute-start | bytes 235016 | tf_op jit(solution)/shard_map/ppermute | solution.py:160
  12.6 18.0 %collective-permute-start.3 = (f32[24,816]{1,0:T(8,128)}, f32[24,816]{1,0:T(8,128)}, u32[]{:S(2)}, u32[]{:S(2)}) collective-permute-start(f32[24,816]{1,0:T(8,128)} %pad_maximum_fusion.3), channel_id=1, source_target_pairs={{1,0},{2,1},{3,2},{0,3},{5,4},{6,5},{7,6},{4,7},{9,8},{10,9},{11,1... | collective-permute-start | bytes 235016 | tf_op jit(solution)/shard_map/ppermute | solution.py:161
  14.9 3.4 %copy-start.4 = (s32[6,6]{1,0:T(8,128)S(1)}, s32[6,6]{1,0:T(8,128)}, u32[]{:S(2)}) copy-start(s32[6,6]{1,0:T(8,128)} %param.9) | copy-start | bytes 436
  21.6 3.3 %copy-start.5 = (s32[66]{0:T(128)S(1)}, s32[66]{0:T(128)}, u32[]{:S(2)}) copy-start(s32[66]{0:T(128)} %and_select_fusion) | copy-start | bytes 796
  27.2 2.3 %copy-start.3 = (s32[24,48]{1,0:T(8,128)S(1)}, s32[24,48]{1,0:T(8,128)}, u32[]{:S(2)}) copy-start(s32[24,48]{1,0:T(8,128)} %param.7) | copy-start | bytes 13828
  31.6 2.2 %copy-start = (f32[24,48,792]{2,1,0:T(8,128)S(1)}, f32[24,48,792]{2,1,0:T(8,128)}, u32[]{:S(2)}) copy-start(f32[24,48,792]{2,1,0:T(8,128)} %refs_0_.1) | copy-start | bytes 10948612

commit v2 on v1

--- a/solution.py
+++ b/solution.py
@@ -19,30 +19,78 @@
     count, length = lax.axis_size(axis), array.shape[dim]
     up = [(i, (i + 1) % count) for i in range(count)]
     down = [(j, i) for i, j in up]
-    last = lax.index_in_dim(array, length - 1, dim, keepdims=False)
-    first = lax.index_in_dim(array, 0, dim, keepdims=False)
+    last = lax.index_in_dim(array, length - 1, dim, keepdims=dim > 0)
+    first = lax.index_in_dim(array, 0, dim, keepdims=dim > 0)
     return last, first, up, down
 
 
+def fold_kernel(chan, blocks_ref, cube_ref, out_ref, natural_ref, rows_ref, ahead_ref, back_ref):
+    whole = chan // ROWS * ROWS
+    count = blocks_ref.shape[0]
+    total = chan * chan
+    for first in range(0, total, LANES):
+        length = min(LANES, total - first)
+        piece = cube_ref[:, first : first + length].astype(jnp.float32)
+        if length < LANES:
+            piece = jnp.concatenate([piece, jnp.zeros((chan, LANES - length), jnp.float32)], axis=1)
+        piece = jnp.concatenate([piece, jnp.zeros((LANES - chan, LANES), jnp.float32)], axis=0)
+        natural_ref[first : first + LANES] = piece.T
+    block_of = lax.broadcasted_iota(jnp.int32, ahead_ref.shape[1:], 0) // BLK
+    for one in range(count):
+        ahead = jnp.zeros(block_of.shape, jnp.float32)
+        back = ahead
+        for other in range(count):
+            ahead = jnp.where(block_of == other, (blocks_ref[one, other] > 0).astype(jnp.float32), ahead)
+            back = jnp.where(block_of == other, (blocks_ref[other, one] > 0).astype(jnp.float32), back)
+        ahead_ref[one] = ahead
+        back_ref[one] = back
+
+    def forward(i, start, stop):
+        return natural_ref[i * chan + start : i * chan + stop] * ahead_ref[i // BLK, start:stop]
+
+    def backward(i, start, stop):
+        taken = natural_ref[pl.ds(start * chan + i, stop - start, stride=chan), :]
+        return taken * back_ref[i // BLK, start:stop]
+
+    at = 0
+    for i in range(whole):
+        start = i // ROWS * ROWS
+        rows_ref[at : at + ROWS] = forward(i, start, start + ROWS)
+        at += ROWS
+        start += ROWS
+        if start < whole:
+            rows_ref[at : at + whole - start] = forward(i, start, whole) + backward(i, start, whole)
+            at += whole - start
+    for i in range(whole, chan):
+        rows_ref[at : at + whole] = forward(i, 0, whole) + backward(i, 0, whole)
+        at += whole
+    for i in range(whole, chan):
+        rows_ref[at : at + ROWS] = jnp.zeros((ROWS, LANES), jnp.float32)
+        rows_ref[at : at + chan - whole] = forward(i, whole, chan)
+        at += ROWS
+    rows_ref[at:] = jnp.zeros((rows_ref.shape[0] - at, LANES), jnp.float32)
+    for first in range(0, rows_ref.shape[0], LANES):
+        turned = rows_ref[first : first + LANES].T
+        out_ref[:, first : first + LANES] = turned[: out_ref.shape[0]].astype(jnp.bfloat16)
+
+
 def folded_kernel(coal_kernel, block_mask, chan):
-    of_bin = jnp.repeat(jnp.repeat(block_mask, BLK, axis=0), BLK, axis=1)
-    cube = coal_kernel.astype(jnp.float32).T.reshape(chan, chan, chan)
-    cube = jnp.where(of_bin[None] > 0, cube, 0.0)
-    both = cube + cube.transpose(0, 2, 1)
-    whole = chan // ROWS * ROWS
-    at = jnp.arange(chan)
-    same = (at[:, None] // ROWS == at[None, :] // ROWS)[None]
-    used = jnp.where(same, cube, both).astype(jnp.bfloat16)
-    parts = []
-    for first in range(0, whole, ROWS):
-        piece = used[:, first : first + ROWS, first:whole]
-        parts.append(piece.reshape(chan, -1))
-    if whole < chan:
-        parts.append(used[:, whole:, :whole].reshape(chan, -1))
-        corner = jnp.pad(used[:, whole:, whole:], ((0, 0), (0, 0), (0, ROWS - (chan - whole))))
-        parts.append(corner.reshape(chan, -1))
-    flat = jnp.concatenate(parts, axis=1)
-    return jnp.pad(flat, ((0, round_up(chan, ROWS) - chan), (0, round_up(flat.shape[1], DEPTH) - flat.shape[1])))
+    depth = round_up(len(pair_blocks(chan)) * ROWS, DEPTH)
+    blocks = block_mask.shape[0]
+    return pl.pallas_call(
+        lambda *refs: fold_kernel(chan, *refs),
+        out_shape=jax.ShapeDtypeStruct((round_up(chan, ROWS), depth), jnp.bfloat16),
+        in_specs=[pl.BlockSpec(memory_space=pltpu.SMEM), pl.BlockSpec(memory_space=pltpu.VMEM)],
+        out_specs=pl.BlockSpec(memory_space=pltpu.VMEM),
+        scratch_shapes=[
+            pltpu.VMEM((round_up(chan * chan, LANES), LANES), jnp.float32),
+            pltpu.VMEM((depth, LANES), jnp.float32),
+            pltpu.VMEM((blocks, round_up(chan, 8), LANES), jnp.float32),
+            pltpu.VMEM((blocks, round_up(chan, 8), LANES), jnp.float32),
+        ],
+        cost_estimate=pl.CostEstimate(flops=2**25, bytes_accessed=2**22, transcendentals=0),
+        compiler_params=pltpu.CompilerParams(vmem_limit_bytes=16 * 2**20),
+    )(block_mask, coal_kernel.T)
 
 
 def pair_blocks(chan):
@@ -154,11 +202,10 @@
     chan = width // levels
     sides = []
     for axis, dim in (("gx", 0), ("gy", 1)):
-        shape = (size_y, -1) if dim == 0 else (size_x, 1, -1)
         last, first, up, down = edges(hydro, axis, dim)
         wlast, wfirst, _, _ = edges(winds, axis, dim)
-        sides.append(lax.ppermute(jnp.concatenate([last, wlast], axis=1), axis, up).reshape(shape))
-        sides.append(lax.ppermute(jnp.concatenate([first, wfirst], axis=1), axis, down).reshape(shape))
+        sides.append(lax.ppermute(jnp.concatenate([last, wlast], axis=-1), axis, up))
+        sides.append(lax.ppermute(jnp.concatenate([first, wfirst], axis=-1), axis, down))
     fold = folded_kernel(coal_kernel, block_mask, chan)
     onto = (jnp.arange(levels)[:, None] == jnp.arange(width)[None, :] // chan).astype(jnp.bfloat16)
     onto = jnp.concatenate([onto] * 3, axis=0)

time: 63.2 us -> 50 us (0.79)
  local copies, waits for them, and re-layouts: 18 us -> 8.39 us
  other arithmetic: 7.7 us -> 0.43 us
  waiting for transfers between devices: 0.01 us -> 2.62 us
  Pallas kernels: 29.1 us -> 30.2 us
    reshape x9 -> x0, local copies, waits for them, and re-layouts: 5.07 us -> none  [the longest x1 2.22 us: folded_kernel(): cube = coal_kernel.astype(jnp.float32).T.reshape(chan, chan, chan)]
    select_n x1 -> x0, local copies, waits for them, and re-layouts: 3.27 us -> none  [folded_kernel(): cube = jnp.where(of_bin[None] > 0, cube, 0.0)]
    ppermute x4, waiting for transfers between devices: 0.01 us -> 2.62 us  [the longest x2 2.08 us: per_device(): lax.ppermute(jnp.concatenate([first, wfirst], axis=-1), axis, down)]
    select_n x2 -> x0, other arithmetic: 2.18 us -> none  [the longest x1 1.6 us: folded_kernel(): cube = jnp.where(of_bin[None] > 0, cube, 0.0)]
    convert_element_type x1 -> x0, other arithmetic: 2.02 us -> none  [folded_kernel(): used = jnp.where(same, cube, both).astype(jnp.bfloat16)]
    concatenate x4, other arithmetic: 2.23 us -> 0.38 us  [the longest x2 0.19 us: per_device(): jnp.concatenate([last, wlast], axis=-1)]
    gt x4 -> x0, local copies, waits for them, and re-layouts: 1.63 us -> none  [folded_kernel(): cube = jnp.where(of_bin[None] > 0, cube, 0.0)]
    slice x10 -> x2, local copies, waits for them, and re-layouts: 2.76 us -> 1.45 us  [edges(): first = lax.index_in_dim(array, 0, dim, keepdims=dim > 0)]
  transfers between devices with their start and end apart: 4 -> 4, of which waited for: 0 -> 2; matrix products, arithmetic and copies ran while one was open for 34% -> 4% of each run, Pallas kernels for 0% -> 3%
where the time goes in v2:
time: 50 us; the launch traced here: 49.6 us
  Pallas kernels  30.2 us (60%)
  local copies, waits for them, and re-layouts  8.39 us (17%)
  starting transfers between devices  7.84 us (16%)
  waiting for transfers between devices  2.62 us (5%)
    pallas_call x1, Pallas kernels, per_device(): pl.pallas_call(lambda *refs: step_kernel(levels, chan, *refs), out_shape=...  29 us
    unnamed x7, local copies, waits for them, and re-layouts  5.12 us
    ppermute x2, starting transfers between devices, per_device(): lax.ppermute(jnp.concatenate([first, wfirst], axis=-1), axis, down)  5.08 us
    ppermute x2, starting transfers between devices, per_device(): lax.ppermute(jnp.concatenate([last, wlast], axis=-1), axis, up)  2.76 us
    ppermute x2, waiting for transfers between devices, per_device(): lax.ppermute(jnp.concatenate([first, wfirst], axis=-1), axis, down)  2.08 us
    slice x2, local copies, waits for them, and re-layouts, edges(): first = lax.index_in_dim(array, 0, dim, keepdims=dim > 0)  1.45 us
    pallas_call x1, Pallas kernels, folded_kernel(): pl.pallas_call(lambda *refs: fold_kernel(chan, *refs), out_shape=jax.Shap...  1.27 us
    squeeze x2, local copies, waits for them, and re-layouts, edges(): first = lax.index_in_dim(array, 0, dim, keepdims=dim > 0)  1.03 us
  transfers between devices with their start and end apart: 4, of which 2 were waited for; matrix products, arithmetic and copies ran while one was open for 4% of the time, Pallas kernels for 3%

profile of v2, /device:TPU:0, one launch (start us, length us, event | category | flops | bytes accessed | tf_op | source)
XLA Modules:
  0.0 49.6 jit_solution(16676408242783996756)
XLA Ops:
  0.0 1.4 %fusion.3 = (f32[24,1,792]{2,1,0:T(1,128)S(1)}, f32[24,1,792]{2,1,0:T(1,128)S(1)}) fusion(f32[24,48,792]{2,1,0:T(8,128)} %refs_0_.3), kind=kLoop, calls=%fused_computation.17 | loop fusion | bytes 304128 | tf_op jit(solution)/shard_map/slice | solution.py:23
  1.4 1.2 %copy.10.refs_1_ = f32[24,48,24]{2,1,0:T(8,128)S(1)} copy(f32[24,48,24]{1,2,0:T(8,128)} %param.6) | data formatting | bytes 221184 | tf_op args[1]
  2.7 0.1 pad_maximum_fusion.2
  2.8 0.5 %collective-permute-start.2 = (f32[24,1,816]{2,1,0:T(1,128)S(1)}, f32[24,1,816]{2,1,0:T(1,128)S(1)}, u32[]{:S(2)}, u32[]{:S(2)}) collective-permute-start(f32[24,1,816]{2,1,0:T(1,128)S(1)} %pad_maximum_fusion.2), channel_id=1, source_target_pairs={{0,1},{1,2},{2,3},{3,0},{4,5},{5,6},{6,7},{7,4},{8,9},{9,10},{10,1... | collective-permute-start | bytes 235016 | tf_op jit(solution)/shard_map/ppermute | solution.py:207
  3.3 0.1 pad_maximum_fusion.3
  3.4 2.0 %collective-permute-start.3 = (f32[24,1,816]{2,1,0:T(1,128)S(1)}, f32[24,1,816]{2,1,0:T(1,128)S(1)}, u32[]{:S(2)}, u32[]{:S(2)}) collective-permute-start(f32[24,1,816]{2,1,0:T(1,128)S(1)} %pad_maximum_fusion.3), channel_id=1, source_target_pairs={{1,0},{2,1},{3,2},{0,3},{5,4},{6,5},{7,6},{4,7},{9,8},{10,9},{11,1... | collective-permute-start | bytes 235016 | tf_op jit(solution)/shard_map/ppermute | solution.py:208
  5.4 1.0 %slice_bitcast_fusion = (f32[48,792]{1,0:T(8,128)S(1)}, f32[48,792]{1,0:T(8,128)S(1)}) fusion(f32[24,48,792]{2,1,0:T(8,128)} %refs_0_.3), kind=kLoop, calls=%fused_computation.2 | loop fusion | bytes 608256 | tf_op jit(solution)/shard_map/squeeze | solution.py:23
  6.5 0.1 pad_maximum_fusion
  6.5 2.3 %collective-permute-start = (f32[48,816]{1,0:T(8,128)S(1)}, f32[48,816]{1,0:T(8,128)S(1)}, u32[]{:S(2)}, u32[]{:S(2)}) collective-permute-start(f32[48,816]{1,0:T(8,128)S(1)} %pad_maximum_fusion), channel_id=1, source_target_pairs={{0,4},{4,8},{8,12},{12,16},{16,20},{20,24},{24,28},{28,0},{1,5},{5... | collective-permute-start | bytes 470024 | tf_op jit(solution)/shard_map/ppermute | solution.py:207
  8.8 0.1 pad_maximum_fusion.1
  8.9 3.1 %collective-permute-start.1 = (f32[48,816]{1,0:T(8,128)S(1)}, f32[48,816]{1,0:T(8,128)S(1)}, u32[]{:S(2)}, u32[]{:S(2)}) collective-permute-start(f32[48,816]{1,0:T(8,128)S(1)} %pad_maximum_fusion.1), channel_id=1, source_target_pairs={{4,0},{8,4},{12,8},{16,12},{20,16},{24,20},{28,24},{0,28},{5,1},{9... | collective-permute-start | bytes 470024 | tf_op jit(solution)/shard_map/ppermute | solution.py:208
  12.0 0.8 %reshape.29.refs_6_ = s32[9,1,128]{2,1,0:T(1,128)S(1)} reshape(s32[24,48]{1,0:T(8,128)} %param.7) | data formatting | bytes 9216 | tf_op jit(solution)/shard_map/reshape | solution.py:212
  12.7 0.0 copy-start.1
  12.8 1.1 %copy-done.1 = bf16[4356,66]{0,1:T(8,128)(2,1)S(1)} copy-done((bf16[4356,66]{0,1:T(8,128)(2,1)S(1)}, bf16[4356,66]{0,1:T(8,128)(2,1)}, u32[]{:S(2)}) %copy-start.1) | copy-done | bytes 575016
  13.8 0.0 copy-start.2
  13.8 0.7 %copy-done.2 = s32[6,6]{1,0:T(8,128)S(1)} copy-done((s32[6,6]{1,0:T(8,128)S(1)}, s32[6,6]{1,0:T(8,128)}, u32[]{:S(2)}) %copy-start.2) | copy-done | bytes 168
  14.5 1.3 %shard_map.55.refs_8_ = bf16[80,2816]{1,0:T(8,128)(2,1)S(1)} custom-call(s32[6,6]{1,0:T(8,128)S(1)} %copy-done.2, bf16[66,4356]{1,0:T(8,128)(2,1)S(1)} %bitcast.10), custom_call_target="tpu_custom_call" | custom-call | flops 33554432 | bytes 4194304 | tf_op jit(solution)/shard_map/pallas_call | solution.py:80
  15.8 0.0 collective-permute-done.2.refs_4_
  15.8 0.0 collective-permute-done.3.refs_5_
  15.9 0.5 %collective-permute-done.refs_2_ = f32[48,816]{1,0:T(8,128)S(1)} collective-permute-done((f32[48,816]{1,0:T(8,128)S(1)}, f32[48,816]{1,0:T(8,128)S(1)}, u32[]{:S(2)}, u32[]{:S(2)}) %collective-permute-start) | collective-permute-done | bytes 156704 | tf_op jit(solution)/shard_map/ppermute | solution.py:207
  16.4 2.1 %collective-permute-done.1.refs_3_ = f32[48,816]{1,0:T(8,128)S(1)} collective-permute-done((f32[48,816]{1,0:T(8,128)S(1)}, f32[48,816]{1,0:T(8,128)S(1)}, u32[]{:S(2)}, u32[]{:S(2)}) %collective-permute-start.1) | collective-permute-done | bytes 156704 | tf_op jit(solution)/shard_map/ppermute | solution.py:208
  18.5 0.0 copy-start
  18.5 2.2 %copy-done = f32[24,48,792]{2,1,0:T(8,128)S(1)} copy-done((f32[24,48,792]{2,1,0:T(8,128)S(1)}, f32[24,48,792]{2,1,0:T(8,128)}, u32[]{:S(2)}) %copy-start) | copy-done | bytes 3649560
  20.6 29.0 %shard_map.56 = f32[1152,792]{1,0:T(8,128)} custom-call(f32[24,48,792]{2,1,0:T(8,128)S(1)} %copy-done, f32[24,48,24]{2,1,0:T(8,128)S(1)} %copy.10.refs_1_, f32[48,816]{1,0:T(8,128)S(1)} %collective-permute-done.refs_2_, f32[48,816]{1,0:T(8,128)S(1)} %collective-permute-done.1.refs_3_, f32[24,1,816]{2,1,0:T(1,128)S(1)} %collective-permute-done.2.refs_4_, ...), custom_call_target="tpu_custom_call" | custom-call | tf_op jit(solution)/shard_map/pallas_call | solution.py:214
  (5 shorter events, 0.1 us)
Async XLA Ops:
  2.8 13.1 %collective-permute-start.2 = (f32[24,1,816]{2,1,0:T(1,128)S(1)}, f32[24,1,816]{2,1,0:T(1,128)S(1)}, u32[]{:S(2)}, u32[]{:S(2)}) collective-permute-start(f32[24,1,816]{2,1,0:T(1,128)S(1)} %pad_maximum_fusion.2), channel_id=1, source_target_pairs={{0,1},{1,2},{2,3},{3,0},{4,5},{5,6},{6,7},{7,4},{8,9},{9,10},{10,1... | collective-permute-start | bytes 235016 | tf_op jit(solution)/shard_map/ppermute | solution.py:207
  3.4 12.5 %collective-permute-start.3 = (f32[24,1,816]{2,1,0:T(1,128)S(1)}, f32[24,1,816]{2,1,0:T(1,128)S(1)}, u32[]{:S(2)}, u32[]{:S(2)}) collective-permute-start(f32[24,1,816]{2,1,0:T(1,128)S(1)} %pad_maximum_fusion.3), channel_id=1, source_target_pairs={{1,0},{2,1},{3,2},{0,3},{5,4},{6,5},{7,6},{4,7},{9,8},{10,9},{11,1... | collective-permute-start | bytes 235016 | tf_op jit(solution)/shard_map/ppermute | solution.py:208
  6.5 9.9 %collective-permute-start = (f32[48,816]{1,0:T(8,128)S(1)}, f32[48,816]{1,0:T(8,128)S(1)}, u32[]{:S(2)}, u32[]{:S(2)}) collective-permute-start(f32[48,816]{1,0:T(8,128)S(1)} %pad_maximum_fusion), channel_id=1, source_target_pairs={{0,4},{4,8},{8,12},{12,16},{16,20},{20,24},{24,28},{28,0},{1,5},{5... | collective-permute-start | bytes 470024 | tf_op jit(solution)/shard_map/ppermute | solution.py:207
  8.9 9.6 %collective-permute-start.1 = (f32[48,816]{1,0:T(8,128)S(1)}, f32[48,816]{1,0:T(8,128)S(1)}, u32[]{:S(2)}, u32[]{:S(2)}) collective-permute-start(f32[48,816]{1,0:T(8,128)S(1)} %pad_maximum_fusion.1), channel_id=1, source_target_pairs={{4,0},{8,4},{12,8},{16,12},{20,16},{24,20},{28,24},{0,28},{5,1},{9... | collective-permute-start | bytes 470024 | tf_op jit(solution)/shard_map/ppermute | solution.py:208
  12.7 1.1 %copy-start.1 = (bf16[4356,66]{0,1:T(8,128)(2,1)S(1)}, bf16[4356,66]{0,1:T(8,128)(2,1)}, u32[]{:S(2)}) copy-start(bf16[4356,66]{0,1:T(8,128)(2,1)} %param.8) | copy-start | bytes 1724980
  13.8 0.7 %copy-start.2 = (s32[6,6]{1,0:T(8,128)S(1)}, s32[6,6]{1,0:T(8,128)}, u32[]{:S(2)}) copy-start(s32[6,6]{1,0:T(8,128)} %refs_0_.2) | copy-start | bytes 436
  18.5 2.2 %copy-start = (f32[24,48,792]{2,1,0:T(8,128)S(1)}, f32[24,48,792]{2,1,0:T(8,128)}, u32[]{:S(2)}) copy-start(f32[24,48,792]{2,1,0:T(8,128)} %refs_0_.3) | copy-start | bytes 10948612

commit v3 on v2

--- a/solution.py
+++ b/solution.py
@@ -15,13 +15,93 @@
     return (value + unit - 1) // unit * unit
 
 
-def edges(array, axis, dim):
-    count, length = lax.axis_size(axis), array.shape[dim]
-    up = [(i, (i + 1) % count) for i in range(count)]
-    down = [(j, i) for i, j in up]
-    last = lax.index_in_dim(array, length - 1, dim, keepdims=dim > 0)
-    first = lax.index_in_dim(array, 0, dim, keepdims=dim > 0)
-    return last, first, up, down
+def halo_kernel(axes, q_ref, w_ref, left_ref, right_ref, below_ref, above_ref, x_rows, y_rows, x_out, y_out, x_in, y_in,
+                near_sem, send_sem, recv_sem):
+    size_x, size_y, width = q_ref.shape
+    faces = w_ref.shape[2]
+    wide = round_up(width, LANES)
+    near = [
+        pltpu.make_async_copy(q_ref.at[size_x - 1], x_rows.at[0], near_sem.at[0]),
+        pltpu.make_async_copy(q_ref.at[0], x_rows.at[1], near_sem.at[1]),
+        pltpu.make_async_copy(q_ref.at[:, size_y - 8 : size_y], y_rows.at[0], near_sem.at[2]),
+        pltpu.make_async_copy(q_ref.at[:, 0:8], y_rows.at[1], near_sem.at[3]),
+    ]
+    for copy in near:
+        copy.start()
+    me = [lax.axis_index(axis) for axis, _ in axes]
+    sides = []
+    for spot, (_, count) in enumerate(axes):
+        for move in (1, count - 1):
+            place = list(me)
+            place[spot] = lax.rem(me[spot] + move, count)
+            sides.append(tuple(place))
+    barrier = pltpu.get_barrier_semaphore()
+    for side in sides:
+        pl.semaphore_signal(barrier, inc=1, device_id=side, device_id_type=pl.DeviceIdType.MESH)
+    x_out[...] = jnp.zeros_like(x_out)
+    y_out[...] = jnp.zeros_like(y_out)
+    for copy in near:
+        copy.wait()
+    for k, x in enumerate((size_x - 1, 0)):
+        x_out[k, :, :width] = x_rows[k]
+        x_out[k, :, wide : wide + faces] = w_ref[x]
+
+    def pick(x, carry):
+        for k, (row, y) in enumerate(((7, size_y - 1), (0, 0))):
+            y_out[k, x, :, :width] = y_rows[k, x][row : row + 1]
+            y_out[k, x, :, wide : wide + faces] = w_ref[x][y : y + 1]
+        return carry
+
+    lax.fori_loop(0, size_x, pick, 0)
+    pl.semaphore_wait(barrier, len(sides))
+    moves = []
+    for k, side in enumerate(sides):
+        out, into = (x_out, x_in) if k < 2 else (y_out, y_in)
+        moves.append(
+            pltpu.make_async_remote_copy(
+                src_ref=out.at[k % 2],
+                dst_ref=into.at[k % 2],
+                send_sem=send_sem.at[k],
+                recv_sem=recv_sem.at[k],
+                device_id=side,
+                device_id_type=pl.DeviceIdType.MESH,
+            )
+        )
+    for move in moves:
+        move.start()
+    for move in moves:
+        move.wait()
+    left_ref[...] = x_in[0]
+    right_ref[...] = x_in[1]
+    below_ref[...] = y_in[0]
+    above_ref[...] = y_in[1]
+
+
+def halos(hydro, winds):
+    size_x, size_y, width = hydro.shape
+    long = round_up(width, LANES) + round_up(winds.shape[2], LANES)
+    axes = tuple((axis, lax.axis_size(axis)) for axis in ("gx", "gy"))
+    along_x, along_y = (size_y, long), (size_x, 1, long)
+    return pl.pallas_call(
+        lambda *refs: halo_kernel(axes, *refs),
+        out_shape=[jax.ShapeDtypeStruct(shape, jnp.float32) for shape in (along_x, along_x, along_y, along_y)],
+        in_specs=[pl.BlockSpec(memory_space=pl.ANY), pl.BlockSpec(memory_space=pltpu.VMEM)],
+        out_specs=[pl.BlockSpec(memory_space=pltpu.VMEM)] * 4,
+        scratch_shapes=[
+            pltpu.VMEM((2, size_y, width), jnp.float32),
+            pltpu.VMEM((2, size_x, 8, width), jnp.float32),
+            pltpu.VMEM((2,) + along_x, jnp.float32),
+            pltpu.VMEM((2,) + along_y, jnp.float32),
+            pltpu.VMEM((2,) + along_x, jnp.float32),
+            pltpu.VMEM((2,) + along_y, jnp.float32),
+            pltpu.SemaphoreType.DMA((4,)),
+            pltpu.SemaphoreType.DMA((4,)),
+            pltpu.SemaphoreType.DMA((4,)),
+        ],
+        compiler_params=pltpu.CompilerParams(
+            collective_id=0, has_side_effects=True, vmem_limit_bytes=56 * 2**20
+        ),
+    )(hydro, winds)
 
 
 def fold_kernel(chan, blocks_ref, cube_ref, out_ref, natural_ref, rows_ref, ahead_ref, back_ref):
@@ -109,10 +189,25 @@
     return jnp.concatenate([high, middle, low], axis=1)
 
 
-def step_kernel(levels, chan, q_ref, w_ref, left_ref, right_ref, below_ref, above_ref, mask_ref, spread_ref, fold_ref,
-                out_ref, turned_ref, back_ref, flux_ref, tall_ref, wtall_ref):
+def step_kernel(levels, chan, q_hbm, w_ref, left_ref, right_ref, below_ref, above_ref, mask_ref, spread_ref, fold_ref,
+                out_hbm, turned_ref, back_ref, flux_ref, tall_ref, wtall_ref, q_ref, out_ref, in_sem, out_sem):
     size_x, size_y, width = q_ref.shape
+
+    def fetch(x):
+        return pltpu.make_async_copy(q_hbm.at[x], q_ref.at[x], in_sem.at[x])
+
+    def keep(block):
+        rows = pl.ds(pl.multiple_of(block * LANES, LANES), LANES)
+        return pltpu.make_async_copy(out_ref.at[rows], out_hbm.at[rows], out_sem.at[block])
+
+    def start_fetch(x, carry):
+        fetch(x).start()
+        return carry
+
+    lax.fori_loop(0, size_x, start_fetch, 0)
+    fetch(0).wait()
     top = 8
+    wide_at = round_up(width, LANES)
 
     def spread(face):
         return jnp.dot(three_parts(face), spread_ref[...], preferred_element_type=jnp.float32)
@@ -121,7 +216,7 @@
         return jnp.maximum(face, 0.0) * before + jnp.minimum(face, 0.0) * after
 
     u_first = w_ref[0][:, :levels]
-    face = spread(0.5 * (left_ref[:, width : width + levels] + u_first))
+    face = spread(0.5 * (left_ref[:, wide_at : wide_at + levels] + u_first))
     flux_ref[...] = upwind(face, left_ref[:, :width], q_ref[0])
 
     def advect(x, q_next, u_next):
@@ -131,8 +226,8 @@
         tall_ref[top - 1 : top] = below_ref[x][:, :width]
         tall_ref[top + size_y : top + size_y + 1] = above_ref[x][:, :width]
         wtall_ref[top : top + size_y] = winds
-        wtall_ref[top - 1 : top] = below_ref[x][:, width:]
-        wtall_ref[top + size_y : top + size_y + 1] = above_ref[x][:, width:]
+        wtall_ref[top - 1 : top] = below_ref[x][:, wide_at : wide_at + 2 * levels]
+        wtall_ref[top + size_y : top + size_y + 1] = above_ref[x][:, wide_at : wide_at + 2 * levels]
         v = winds[:, levels:]
         v_before = wtall_ref[top - 1 : top - 1 + size_y][:, levels:]
         v_after = wtall_ref[top + 1 : top + 1 + size_y][:, levels:]
@@ -148,11 +243,12 @@
         out_ref[pl.ds(pl.multiple_of(x * size_y, 8), size_y), :] = result
 
     def advect_inner(x, carry):
+        fetch(x + 1).wait()
         advect(x, q_ref[x + 1], w_ref[x + 1][:, :levels])
         return carry
 
     lax.fori_loop(0, size_x - 1, advect_inner, 0)
-    advect(size_x - 1, right_ref[:, :width], right_ref[:, width : width + levels])
+    advect(size_x - 1, right_ref[:, :width], right_ref[:, wide_at : wide_at + levels])
 
     runs = pair_blocks(chan)
     per_chunk = DEPTH // ROWS
@@ -190,22 +286,25 @@
                 kept = rounded[:chan, half * LANES : (half + 1) * LANES]
                 back_ref[s : s + chan] = jnp.where(cloudy, kept, 0.0)
         out_ref[rows, :] = advected + back_ref[...].T[:, :width]
+        keep(block).start()
         return carry
 
     back_ref[...] = jnp.zeros_like(back_ref)
-    lax.fori_loop(0, size_x * size_y // LANES, collide, 0)
+    blocks = size_x * size_y // LANES
+    lax.fori_loop(0, blocks, collide, 0)
+
+    def finish(block, carry):
+        keep(block).wait()
+        return carry
+
+    lax.fori_loop(0, blocks, finish, 0)
 
 
 def per_device(hydro, winds, cloud_mask, coal_kernel, block_mask):
     size_x, size_y, width = hydro.shape
     levels = winds.shape[2] // 2
     chan = width // levels
-    sides = []
-    for axis, dim in (("gx", 0), ("gy", 1)):
-        last, first, up, down = edges(hydro, axis, dim)
-        wlast, wfirst, _, _ = edges(winds, axis, dim)
-        sides.append(lax.ppermute(jnp.concatenate([last, wlast], axis=-1), axis, up))
-        sides.append(lax.ppermute(jnp.concatenate([first, wfirst], axis=-1), axis, down))
+    sides = halos(hydro, winds)
     fold = folded_kernel(coal_kernel, block_mask, chan)
     onto = (jnp.arange(levels)[:, None] == jnp.arange(width)[None, :] // chan).astype(jnp.bfloat16)
     onto = jnp.concatenate([onto] * 3, axis=0)
@@ -214,16 +313,20 @@
     result = pl.pallas_call(
         lambda *refs: step_kernel(levels, chan, *refs),
         out_shape=jax.ShapeDtypeStruct((size_x * size_y, width), jnp.float32),
-        in_specs=[pl.BlockSpec(memory_space=pltpu.VMEM)] * 9,
-        out_specs=pl.BlockSpec(memory_space=pltpu.VMEM),
+        in_specs=[pl.BlockSpec(memory_space=pl.ANY)] + [pl.BlockSpec(memory_space=pltpu.VMEM)] * 8,
+        out_specs=pl.BlockSpec(memory_space=pl.ANY),
         scratch_shapes=[
             pltpu.VMEM((long, LANES), jnp.float32),
             pltpu.VMEM((long, LANES), jnp.float32),
             pltpu.VMEM((size_y, width), jnp.float32),
             pltpu.VMEM((size_y + 16, width), jnp.float32),
             pltpu.VMEM((size_y + 16, 2 * levels), jnp.float32),
+            pltpu.VMEM((size_x, size_y, width), jnp.float32),
+            pltpu.VMEM((size_x * size_y, width), jnp.float32),
+            pltpu.SemaphoreType.DMA((size_x,)),
+            pltpu.SemaphoreType.DMA((size_x * size_y // LANES,)),
         ],
-        compiler_params=pltpu.CompilerParams(vmem_limit_bytes=40 * 2**20),
+        compiler_params=pltpu.CompilerParams(vmem_limit_bytes=56 * 2**20),
     )(hydro, winds, *sides, mask, onto, fold)
     return result.reshape(size_x, size_y, width)
 

time: 50 us -> 53 us (1.060)
  Pallas kernels: 30.2 us -> 46 us
  starting transfers between devices: 7.84 us -> 0 us
  waiting for transfers between devices: 2.62 us -> 0 us
  local copies, waits for them, and re-layouts: 8.39 us -> 5.91 us
    pallas_call x0 -> x1, Pallas kernels: none -> 15.9 us  [halos(): pl.pallas_call(lambda *refs: halo_kernel(axes, *refs), out_shape=[jax.Sha...]
    ppermute x4 -> x0, starting transfers between devices: 7.84 us -> none  [the longest x2 5.08 us: per_device(): lax.ppermute(jnp.concatenate([first, wfirst], axis=-1), axis, down)]
    ppermute x4 -> x0, waiting for transfers between devices: 2.62 us -> none  [the longest x2 2.08 us: per_device(): lax.ppermute(jnp.concatenate([first, wfirst], axis=-1), axis, down)]
    slice x2 -> x0, local copies, waits for them, and re-layouts: 1.45 us -> none  [edges(): first = lax.index_in_dim(array, 0, dim, keepdims=dim > 0)]
    squeeze x2 -> x0, local copies, waits for them, and re-layouts: 1.03 us -> none  [edges(): first = lax.index_in_dim(array, 0, dim, keepdims=dim > 0)]
    concatenate x1, other arithmetic: 0.03 us -> 0.65 us  [per_device(): onto = jnp.concatenate([onto] * 3, axis=0)]
    unnamed x7, local copies, waits for them, and re-layouts: 5.12 us -> 4.54 us
    reshape x1, local copies, waits for them, and re-layouts: 0.79 us -> 1.37 us  [per_device(): mask = cloud_mask.reshape(-1, 1, LANES)]
  transfers between devices with their start and end apart: 4 -> 0, of which waited for: 2 -> 0; matrix products, arithmetic and copies ran while one was open for 4% -> 0% of each run, Pallas kernels for 3% -> 0%
where the time goes in v3:
time: 53 us; the launch traced here: 52.6 us
  Pallas kernels  46 us (87%)
  local copies, waits for them, and re-layouts  5.91 us (11%)
  other arithmetic  0.67 us (1%)
    pallas_call x1, Pallas kernels, per_device(): pl.pallas_call(lambda *refs: step_kernel(levels, chan, *refs), out_shape=...  28.8 us
    pallas_call x1, Pallas kernels, halos(): pl.pallas_call(lambda *refs: halo_kernel(axes, *refs), out_shape=[jax.Sha...  15.9 us
    unnamed x7, local copies, waits for them, and re-layouts  4.54 us
    reshape x1, local copies, waits for them, and re-layouts, per_device(): mask = cloud_mask.reshape(-1, 1, LANES)  1.37 us
    pallas_call x1, Pallas kernels, folded_kernel(): pl.pallas_call(lambda *refs: fold_kernel(chan, *refs), out_shape=jax.Shap...  1.27 us

profile of v3, /device:TPU:0, one launch (start us, length us, event | category | flops | bytes accessed | tf_op | source)
XLA Modules:
  0.0 52.6 jit_solution(13219970845703948365)
XLA Ops:
  0.0 1.4 %reshape.29.refs_6_ = s32[9,1,128]{2,1,0:T(1,128)} reshape(s32[24,48]{1,0:T(8,128)} %param.7) | data formatting | bytes 9216 | tf_op jit(solution)/shard_map/reshape | solution.py:311
  1.4 0.7 %add_convert_fusion.refs_7_ = bf16[36,792]{1,0:T(8,128)(2,1)} fusion(pred[12,792]{1,0:T(8,128)(4,1)S(1)} %iota_compare_fusion), kind=kLoop, calls=%fused_computation | loop fusion | flops 85536 | bytes 66528 | tf_op jit(solution)/shard_map/concatenate | solution.py:310
  2.0 0.0 copy-start.1
  2.0 1.1 %copy-done.1 = bf16[4356,66]{0,1:T(8,128)(2,1)S(1)} copy-done((bf16[4356,66]{0,1:T(8,128)(2,1)S(1)}, bf16[4356,66]{0,1:T(8,128)(2,1)}, u32[]{:S(2)}) %copy-start.1) | copy-done | bytes 575016
  3.1 0.0 copy-start.2
  3.1 0.7 %copy-done.2 = s32[6,6]{1,0:T(8,128)S(1)} copy-done((s32[6,6]{1,0:T(8,128)S(1)}, s32[6,6]{1,0:T(8,128)}, u32[]{:S(2)}) %copy-start.2) | copy-done | bytes 168
  3.8 1.3 %shard_map.56.refs_8_ = bf16[80,2816]{1,0:T(8,128)(2,1)S(1)} custom-call(s32[6,6]{1,0:T(8,128)S(1)} %copy-done.2, bf16[66,4356]{1,0:T(8,128)(2,1)S(1)} %bitcast.2), custom_call_target="tpu_custom_call" | custom-call | flops 33554432 | bytes 4194304 | tf_op jit(solution)/shard_map/pallas_call | solution.py:160
  5.1 0.0 copy-start
  5.1 0.8 %copy-done = bf16[80,2816]{1,0:T(8,128)(2,1)} copy-done((bf16[80,2816]{1,0:T(8,128)(2,1)}, bf16[80,2816]{1,0:T(8,128)(2,1)S(1)}, u32[]{:S(2)}) %copy-start) | copy-done | bytes 450584
  5.9 2.0 %copy.7.refs_1_ = f32[24,48,24]{2,1,0:T(8,128)} copy(f32[24,48,24]{1,2,0:T(8,128)} %param.6) | data formatting | bytes 221184 | tf_op args[1]
  7.9 15.9 %shard_map.55 = (f32[48,1024]{1,0:T(8,128)}, f32[48,1024]{1,0:T(8,128)}, f32[24,1,1024]{2,1,0:T(1,128)}, f32[24,1,1024]{2,1,0:T(1,128)}) custom-call(f32[24,48,792]{2,1,0:T(8,128)} %refs_0_.5, f32[24,48,24]{2,1,0:T(8,128)} %copy.7.refs_1_), custom_call_target="tpu_custom_call" | custom-call | tf_op jit(solution)/shard_map/pallas_call | solution.py:85
  23.8 28.8 %shard_map.57 = f32[1152,792]{1,0:T(8,128)} custom-call(f32[24,48,792]{2,1,0:T(8,128)} %refs_0_.5, f32[24,48,24]{2,1,0:T(8,128)} %copy.7.refs_1_, f32[48,1024]{1,0:T(8,128)} %get-tuple-element.9.refs_2_, f32[48,1024]{1,0:T(8,128)} %get-tuple-element.10.refs_3_, f32[24,1,1024]{2,1,0:T(1,128)} %get-tuple-element.11.refs_4_, ...), custom_call_target="tpu_custom_call" | custom-call | tf_op jit(solution)/shard_map/pallas_call | solution.py:313
  (2 shorter events, 0.0 us)
Async XLA Ops:
  2.0 1.1 %copy-start.1 = (bf16[4356,66]{0,1:T(8,128)(2,1)S(1)}, bf16[4356,66]{0,1:T(8,128)(2,1)}, u32[]{:S(2)}) copy-start(bf16[4356,66]{0,1:T(8,128)(2,1)} %param.8) | copy-start | bytes 1724980
  3.1 0.7 %copy-start.2 = (s32[6,6]{1,0:T(8,128)S(1)}, s32[6,6]{1,0:T(8,128)}, u32[]{:S(2)}) copy-start(s32[6,6]{1,0:T(8,128)} %refs_0_.4) | copy-start | bytes 436
  5.1 0.8 %copy-start = (bf16[80,2816]{1,0:T(8,128)(2,1)}, bf16[80,2816]{1,0:T(8,128)(2,1)S(1)}, u32[]{:S(2)}) copy-start(bf16[80,2816]{1,0:T(8,128)(2,1)S(1)} %shard_map.56.refs_8_) | copy-start | bytes 1351684

commit v4 on v2

--- a/solution.py
+++ b/solution.py
@@ -52,15 +52,28 @@
         taken = natural_ref[pl.ds(start * chan + i, stop - start, stride=chan), :]
         return taken * back_ref[i // BLK, start:stop]
 
+    row = lax.broadcasted_iota(jnp.int32, (ROWS, LANES), 0)
+    half = ROWS // 2
     at = 0
     for i in range(whole):
-        start = i // ROWS * ROWS
-        rows_ref[at : at + ROWS] = forward(i, start, start + ROWS)
-        at += ROWS
-        start += ROWS
+        start = i // ROWS * ROWS + ROWS
         if start < whole:
             rows_ref[at : at + whole - start] = forward(i, start, whole) + backward(i, start, whole)
             at += whole - start
+    for start in range(0, whole, ROWS):
+        for s in range(half):
+            near = (row >= s) & (row < s + half)
+            i, stop = start + s, start + ROWS
+            there = jnp.where(near, forward(i, start, stop), forward(i + half, start, stop))
+            back = jnp.where(near, backward(i, start, stop), backward(i + half, start, stop))
+            same = (row == s) | (row == s + half)
+            rows_ref[at : at + ROWS] = there + jnp.where(same, 0.0, back)
+            at += ROWS
+    for start in range(0, whole, ROWS):
+        for i in range(start, start + half):
+            j = i + half
+            rows_ref[at : at + 1] = forward(i, j, j + 1) + forward(j, i, i + 1)
+            at += 1
     for i in range(whole, chan):
         rows_ref[at : at + whole] = forward(i, 0, whole) + backward(i, 0, whole)
         at += whole
@@ -95,9 +108,11 @@
 
 def pair_blocks(chan):
     whole = chan // ROWS * ROWS
-    runs = [(i, j) for i in range(whole) for j in range(i // ROWS * ROWS, whole, ROWS)]
-    runs += [(i, j) for i in range(whole, chan) for j in range(0, whole, ROWS)]
-    runs += [(i, whole) for i in range(whole, chan)]
+    runs = [(0, i, j) for i in range(whole) for j in range(i // ROWS * ROWS + ROWS, whole, ROWS)]
+    runs += [(1, start + s, start) for start in range(0, whole, ROWS) for s in range(ROWS // 2)]
+    runs += [(2, start, start + ROWS) for start in range(0, whole, 2 * ROWS)]
+    runs += [(0, i, j) for i in range(whole, chan) for j in range(0, whole, ROWS)]
+    runs += [(0, i, whole) for i in range(whole, chan)]
     return runs
 
 
@@ -109,9 +124,23 @@
     return jnp.concatenate([high, middle, low], axis=1)
 
 
-def step_kernel(levels, chan, q_ref, w_ref, left_ref, right_ref, below_ref, above_ref, mask_ref, spread_ref, fold_ref,
-                out_ref, turned_ref, back_ref, flux_ref, tall_ref, wtall_ref):
+def step_kernel(levels, chan, q_hbm, w_ref, left_ref, right_ref, below_ref, above_ref, mask_ref, spread_ref, fold_ref,
+                out_hbm, turned_ref, back_ref, flux_ref, tall_ref, wtall_ref, q_ref, out_ref, in_sem, out_sem):
     size_x, size_y, width = q_ref.shape
+
+    def fetch(x):
+        return pltpu.make_async_copy(q_hbm.at[x], q_ref.at[x], in_sem.at[x])
+
+    def keep(block):
+        rows = pl.ds(pl.multiple_of(block * LANES, LANES), LANES)
+        return pltpu.make_async_copy(out_ref.at[rows], out_hbm.at[rows], out_sem.at[block])
+
+    def start_fetch(x, carry):
+        fetch(x).start()
+        return carry
+
+    lax.fori_loop(0, size_x, start_fetch, 0)
+    fetch(0).wait()
     top = 8
 
     def spread(face):
@@ -148,6 +177,7 @@
         out_ref[pl.ds(pl.multiple_of(x * size_y, 8), size_y), :] = result
 
     def advect_inner(x, carry):
+        fetch(x + 1).wait()
         advect(x, q_ref[x + 1], w_ref[x + 1][:, :levels])
         return carry
 
@@ -158,6 +188,7 @@
     per_chunk = DEPTH // ROWS
     nothing = jnp.zeros((ROWS, LANES), jnp.bfloat16)
     long = turned_ref.shape[0]
+    row = lax.broadcasted_iota(jnp.int32, (ROWS, LANES), 0)
 
     def collide(block, carry):
         rows = pl.ds(pl.multiple_of(block * LANES, LANES), LANES)
@@ -177,9 +208,19 @@
                 halves = []
                 for s, tile in zip(starts, tiles):
                     made = []
-                    for i, j in runs[chunk : chunk + per_chunk]:
-                        one = jnp.broadcast_to(turned_ref[s + i : s + i + 1], (ROWS, LANES)).astype(jnp.bfloat16)
-                        made.append(one * tile[j // ROWS])
+                    for kind, i, j in runs[chunk : chunk + per_chunk]:
+                        if kind == 2:
+                            parts = [tile[k // ROWS].astype(jnp.float32) for k in (i, j)]
+                            parts = [part[: ROWS // 2] * part[ROWS // 2 :] for part in parts]
+                            made.append(jnp.concatenate(parts, axis=0).astype(jnp.bfloat16))
+                            continue
+                        one = jnp.broadcast_to(turned_ref[s + i : s + i + 1], (ROWS, LANES))
+                        if kind == 1:
+                            k = i + ROWS // 2
+                            far = jnp.broadcast_to(turned_ref[s + k : s + k + 1], (ROWS, LANES))
+                            near = (row >= i - j) & (row < i - j + ROWS // 2)
+                            one = jnp.where(near, one, far)
+                        made.append(one.astype(jnp.bfloat16) * tile[j // ROWS])
                     made += [nothing] * (per_chunk - len(made))
                     halves.append(jnp.concatenate(made, axis=0))
                 pairs = jnp.concatenate(halves, axis=1)
@@ -190,10 +231,18 @@
                 kept = rounded[:chan, half * LANES : (half + 1) * LANES]
                 back_ref[s : s + chan] = jnp.where(cloudy, kept, 0.0)
         out_ref[rows, :] = advected + back_ref[...].T[:, :width]
+        keep(block).start()
         return carry
 
     back_ref[...] = jnp.zeros_like(back_ref)
-    lax.fori_loop(0, size_x * size_y // LANES, collide, 0)
+    blocks = size_x * size_y // LANES
+    lax.fori_loop(0, blocks, collide, 0)
+
+    def finish(block, carry):
+        keep(block).wait()
+        return carry
+
+    lax.fori_loop(0, blocks, finish, 0)
 
 
 def per_device(hydro, winds, cloud_mask, coal_kernel, block_mask):
@@ -214,16 +263,20 @@
     result = pl.pallas_call(
         lambda *refs: step_kernel(levels, chan, *refs),
         out_shape=jax.ShapeDtypeStruct((size_x * size_y, width), jnp.float32),
-        in_specs=[pl.BlockSpec(memory_space=pltpu.VMEM)] * 9,
-        out_specs=pl.BlockSpec(memory_space=pltpu.VMEM),
+        in_specs=[pl.BlockSpec(memory_space=pl.ANY)] + [pl.BlockSpec(memory_space=pltpu.VMEM)] * 8,
+        out_specs=pl.BlockSpec(memory_space=pl.ANY),
         scratch_shapes=[
             pltpu.VMEM((long, LANES), jnp.float32),
             pltpu.VMEM((long, LANES), jnp.float32),
             pltpu.VMEM((size_y, width), jnp.float32),
             pltpu.VMEM((size_y + 16, width), jnp.float32),
             pltpu.VMEM((size_y + 16, 2 * levels), jnp.float32),
+            pltpu.VMEM((size_x, size_y, width), jnp.float32),
+            pltpu.VMEM((size_x * size_y, width), jnp.float32),
+            pltpu.SemaphoreType.DMA((size_x,)),
+            pltpu.SemaphoreType.DMA((size_x * size_y // LANES,)),
         ],
-        compiler_params=pltpu.CompilerParams(vmem_limit_bytes=40 * 2**20),
+        compiler_params=pltpu.CompilerParams(vmem_limit_bytes=56 * 2**20),
     )(hydro, winds, *sides, mask, onto, fold)
     return result.reshape(size_x, size_y, width)
 

time: 50 us -> 47.8 us (0.956)
  waiting for transfers between devices: 2.62 us -> 0.57 us
  other arithmetic: 0.43 us -> 1.05 us
  Pallas kernels: 30.2 us -> 29.6 us
    ppermute x2, waiting for transfers between devices: 2.08 us -> 0.57 us  [per_device(): lax.ppermute(jnp.concatenate([first, wfirst], axis=-1), axis, down)]
    pallas_call x1, Pallas kernels: 29 us -> 28.2 us  [per_device(): pl.pallas_call(lambda *refs: step_kernel(levels, chan, *refs), out_shape=...]
    unnamed x7 -> x17, local copies, waits for them, and re-layouts: 5.12 us -> 4.49 us
    concatenate x1, other arithmetic: 0.03 us -> 0.65 us  [per_device(): onto = jnp.concatenate([onto] * 3, axis=0)]
    reshape x1, local copies, waits for them, and re-layouts: 0.79 us -> 1.38 us  [per_device(): mask = cloud_mask.reshape(-1, 1, LANES)]
    ppermute x2, waiting for transfers between devices: 0.54 us -> 0.01 us  [per_device(): lax.ppermute(jnp.concatenate([last, wlast], axis=-1), axis, up)]
  transfers between devices with their start and end apart: 4 -> 4, of which waited for: 2 -> 1; matrix products, arithmetic and copies ran while one was open for 4% -> 7% of each run, Pallas kernels for 3% -> 3%
where the time goes in v4:
time: 47.8 us; the launch traced here: 47.5 us
  Pallas kernels  29.6 us (62%)
  local copies, waits for them, and re-layouts  8.35 us (17%)
  starting transfers between devices  7.84 us (16%)
  other arithmetic  1.05 us (2%)
  waiting for transfers between devices  0.57 us (1%)
    pallas_call x1, Pallas kernels, per_device(): pl.pallas_call(lambda *refs: step_kernel(levels, chan, *refs), out_shape=...  28.2 us
    ppermute x2, starting transfers between devices, per_device(): lax.ppermute(jnp.concatenate([first, wfirst], axis=-1), axis, down)  5.08 us
    unnamed x17, local copies, waits for them, and re-layouts  4.49 us
    ppermute x2, starting transfers between devices, per_device(): lax.ppermute(jnp.concatenate([last, wlast], axis=-1), axis, up)  2.76 us
    slice x2, local copies, waits for them, and re-layouts, edges(): first = lax.index_in_dim(array, 0, dim, keepdims=dim > 0)  1.45 us
    reshape x1, local copies, waits for them, and re-layouts, per_device(): mask = cloud_mask.reshape(-1, 1, LANES)  1.38 us
    pallas_call x1, Pallas kernels, folded_kernel(): pl.pallas_call(lambda *refs: fold_kernel(chan, *refs), out_shape=jax.Shap...  1.36 us
    squeeze x2, local copies, waits for them, and re-layouts, edges(): first = lax.index_in_dim(array, 0, dim, keepdims=dim > 0)  1.03 us
  transfers between devices with their start and end apart: 4, of which 1 were waited for; matrix products, arithmetic and copies ran while one was open for 7% of the time, Pallas kernels for 3%

profile of v4, /device:TPU:0, one launch (start us, length us, event | category | flops | bytes accessed | tf_op | source)
XLA Modules:
  0.0 47.5 jit_solution(10727260766434464502)
XLA Ops:
  0.0 1.4 %fusion.3 = (f32[24,1,792]{2,1,0:T(1,128)S(1)}, f32[24,1,792]{2,1,0:T(1,128)S(1)}) fusion(f32[24,48,792]{2,1,0:T(8,128)} %refs_0_.3), kind=kLoop, calls=%fused_computation.17 | loop fusion | bytes 304128 | tf_op jit(solution)/shard_map/slice | solution.py:23
  1.4 1.2 %copy.10.refs_1_ = f32[24,48,24]{2,1,0:T(8,128)S(1)} copy(f32[24,48,24]{1,2,0:T(8,128)} %param.6) | data formatting | bytes 221184 | tf_op args[1]
  2.6 0.0 copy-start.3
  2.7 0.1 pad_maximum_fusion.2
  2.8 0.5 %collective-permute-start.2 = (f32[24,1,816]{2,1,0:T(1,128)S(1)}, f32[24,1,816]{2,1,0:T(1,128)S(1)}, u32[]{:S(2)}, u32[]{:S(2)}) collective-permute-start(f32[24,1,816]{2,1,0:T(1,128)S(1)} %pad_maximum_fusion.2), channel_id=1, source_target_pairs={{0,1},{1,2},{2,3},{3,0},{4,5},{5,6},{6,7},{7,4},{8,9},{9,10},{10,1... | collective-permute-start | bytes 235016 | tf_op jit(solution)/shard_map/ppermute | solution.py:256
  3.3 0.1 pad_maximum_fusion.3
  3.4 2.0 %collective-permute-start.3 = (f32[24,1,816]{2,1,0:T(1,128)S(1)}, f32[24,1,816]{2,1,0:T(1,128)S(1)}, u32[]{:S(2)}, u32[]{:S(2)}) collective-permute-start(f32[24,1,816]{2,1,0:T(1,128)S(1)} %pad_maximum_fusion.3), channel_id=1, source_target_pairs={{1,0},{2,1},{3,2},{0,3},{5,4},{6,5},{7,6},{4,7},{9,8},{10,9},{11,1... | collective-permute-start | bytes 235016 | tf_op jit(solution)/shard_map/ppermute | solution.py:257
  5.4 1.0 %slice_bitcast_fusion = (f32[48,792]{1,0:T(8,128)S(1)}, f32[48,792]{1,0:T(8,128)S(1)}) fusion(f32[24,48,792]{2,1,0:T(8,128)} %refs_0_.3), kind=kLoop, calls=%fused_computation.2 | loop fusion | bytes 608256 | tf_op jit(solution)/shard_map/squeeze | solution.py:23
  6.5 0.1 pad_maximum_fusion
  6.5 2.3 %collective-permute-start = (f32[48,816]{1,0:T(8,128)S(1)}, f32[48,816]{1,0:T(8,128)S(1)}, u32[]{:S(2)}, u32[]{:S(2)}) collective-permute-start(f32[48,816]{1,0:T(8,128)S(1)} %pad_maximum_fusion), channel_id=1, source_target_pairs={{0,4},{4,8},{8,12},{12,16},{16,20},{20,24},{24,28},{28,0},{1,5},{5... | collective-permute-start | bytes 470024 | tf_op jit(solution)/shard_map/ppermute | solution.py:256
  8.8 0.1 pad_maximum_fusion.1
  8.9 3.1 %collective-permute-start.1 = (f32[48,816]{1,0:T(8,128)S(1)}, f32[48,816]{1,0:T(8,128)S(1)}, u32[]{:S(2)}, u32[]{:S(2)}) collective-permute-start(f32[48,816]{1,0:T(8,128)S(1)} %pad_maximum_fusion.1), channel_id=1, source_target_pairs={{4,0},{8,4},{12,8},{16,12},{20,16},{24,20},{28,24},{0,28},{5,1},{9... | collective-permute-start | bytes 470024 | tf_op jit(solution)/shard_map/ppermute | solution.py:257
  12.0 1.4 %reshape.29.refs_6_ = s32[9,1,128]{2,1,0:T(1,128)} reshape(s32[24,48]{1,0:T(8,128)} %param.7) | data formatting | bytes 9216 | tf_op jit(solution)/shard_map/reshape | solution.py:261
  13.3 0.0 copy-start.1
  13.4 1.1 %copy-done.1 = bf16[4356,66]{0,1:T(8,128)(2,1)S(1)} copy-done((bf16[4356,66]{0,1:T(8,128)(2,1)S(1)}, bf16[4356,66]{0,1:T(8,128)(2,1)}, u32[]{:S(2)}) %copy-start.1) | copy-done | bytes 575016
  14.4 0.0 copy-start.2
  14.4 0.7 %copy-done.2 = s32[6,6]{1,0:T(8,128)S(1)} copy-done((s32[6,6]{1,0:T(8,128)S(1)}, s32[6,6]{1,0:T(8,128)}, u32[]{:S(2)}) %copy-start.2) | copy-done | bytes 168
  15.1 1.4 %shard_map.55.refs_8_ = bf16[80,2304]{1,0:T(8,128)(2,1)S(1)} custom-call(s32[6,6]{1,0:T(8,128)S(1)} %copy-done.2, bf16[66,4356]{1,0:T(8,128)(2,1)S(1)} %bitcast.10), custom_call_target="tpu_custom_call" | custom-call | flops 33554432 | bytes 4194304 | tf_op jit(solution)/shard_map/pallas_call | solution.py:93
  16.5 0.0 copy-start
  16.5 0.7 %copy-done = bf16[80,2304]{1,0:T(8,128)(2,1)} copy-done((bf16[80,2304]{1,0:T(8,128)(2,1)}, bf16[80,2304]{1,0:T(8,128)(2,1)S(1)}, u32[]{:S(2)}) %copy-start) | copy-done | bytes 368664
  17.2 0.6 %add_convert_fusion.refs_7_ = bf16[36,792]{1,0:T(8,128)(2,1)} fusion(pred[12,792]{1,0:T(8,128)(4,1)S(1)} %iota_compare_fusion), kind=kLoop, calls=%fused_computation.4 | loop fusion | flops 85536 | bytes 66528 | tf_op jit(solution)/shard_map/concatenate | solution.py:260
  17.9 0.0 collective-permute-done.2.refs_4_
  17.9 0.0 copy-start.6
  17.9 0.0 collective-permute-done.3.refs_5_
  17.9 0.0 copy-start.7
  17.9 0.0 collective-permute-done.refs_2_
  17.9 0.0 copy-start.4
  17.9 0.6 %collective-permute-done.1.refs_3_ = f32[48,816]{1,0:T(8,128)S(1)} collective-permute-done((f32[48,816]{1,0:T(8,128)S(1)}, f32[48,816]{1,0:T(8,128)S(1)}, u32[]{:S(2)}, u32[]{:S(2)}) %collective-permute-start.1) | collective-permute-done | bytes 156704 | tf_op jit(solution)/shard_map/ppermute | solution.py:257
  18.5 0.0 copy-done.3
  18.5 0.0 copy-done.6
  18.5 0.1 copy-done.7
  18.6 0.0 copy-done.4
  18.6 0.0 copy-start.5
  18.6 0.7 %copy-done.5 = f32[48,816]{1,0:T(8,128)} copy-done((f32[48,816]{1,0:T(8,128)}, f32[48,816]{1,0:T(8,128)S(1)}, u32[]{:S(2)}) %copy-start.5) | copy-done | bytes 156696
  19.3 28.2 %shard_map.56 = f32[1152,792]{1,0:T(8,128)} custom-call(f32[24,48,792]{2,1,0:T(8,128)} %refs_0_.3, f32[24,48,24]{2,1,0:T(8,128)} %copy-done.3, f32[48,816]{1,0:T(8,128)} %copy-done.4, f32[48,816]{1,0:T(8,128)} %copy-done.5, f32[24,1,816]{2,1,0:T(1,128)} %copy-done.6, f32[24,1,816]{2,1,0:T(1,128)} %copy-done.7, s32[9,1,128]{2,1,0:T(1,128)} %reshape.29.refs_6_, ...), custom_call_target="tpu_custom_call" | custom-call | tf_op jit(solution)/shard_map/pallas_call | solution.py:263
  (4 shorter events, 0.1 us)
Async XLA Ops:
  2.6 15.9 %copy-start.3 = (f32[24,48,24]{2,1,0:T(8,128)}, f32[24,48,24]{2,1,0:T(8,128)S(1)}, u32[]{:S(2)}) copy-start(f32[24,48,24]{2,1,0:T(8,128)S(1)} %copy.10.refs_1_) | copy-start | bytes 331780
  2.8 15.1 %collective-permute-start.2 = (f32[24,1,816]{2,1,0:T(1,128)S(1)}, f32[24,1,816]{2,1,0:T(1,128)S(1)}, u32[]{:S(2)}, u32[]{:S(2)}) collective-permute-start(f32[24,1,816]{2,1,0:T(1,128)S(1)} %pad_maximum_fusion.2), channel_id=1, source_target_pairs={{0,1},{1,2},{2,3},{3,0},{4,5},{5,6},{6,7},{7,4},{8,9},{9,10},{10,1... | collective-permute-start | bytes 235016 | tf_op jit(solution)/shard_map/ppermute | solution.py:256
  3.4 14.5 %collective-permute-start.3 = (f32[24,1,816]{2,1,0:T(1,128)S(1)}, f32[24,1,816]{2,1,0:T(1,128)S(1)}, u32[]{:S(2)}, u32[]{:S(2)}) collective-permute-start(f32[24,1,816]{2,1,0:T(1,128)S(1)} %pad_maximum_fusion.3), channel_id=1, source_target_pairs={{1,0},{2,1},{3,2},{0,3},{5,4},{6,5},{7,6},{4,7},{9,8},{10,9},{11,1... | collective-permute-start | bytes 235016 | tf_op jit(solution)/shard_map/ppermute | solution.py:257
  6.5 11.4 %collective-permute-start = (f32[48,816]{1,0:T(8,128)S(1)}, f32[48,816]{1,0:T(8,128)S(1)}, u32[]{:S(2)}, u32[]{:S(2)}) collective-permute-start(f32[48,816]{1,0:T(8,128)S(1)} %pad_maximum_fusion), channel_id=1, source_target_pairs={{0,4},{4,8},{8,12},{12,16},{16,20},{20,24},{24,28},{28,0},{1,5},{5... | collective-permute-start | bytes 470024 | tf_op jit(solution)/shard_map/ppermute | solution.py:256
  8.9 9.6 %collective-permute-start.1 = (f32[48,816]{1,0:T(8,128)S(1)}, f32[48,816]{1,0:T(8,128)S(1)}, u32[]{:S(2)}, u32[]{:S(2)}) collective-permute-start(f32[48,816]{1,0:T(8,128)S(1)} %pad_maximum_fusion.1), channel_id=1, source_target_pairs={{4,0},{8,4},{12,8},{16,12},{20,16},{24,20},{28,24},{0,28},{5,1},{9... | collective-permute-start | bytes 470024 | tf_op jit(solution)/shard_map/ppermute | solution.py:257
  13.3 1.1 %copy-start.1 = (bf16[4356,66]{0,1:T(8,128)(2,1)S(1)}, bf16[4356,66]{0,1:T(8,128)(2,1)}, u32[]{:S(2)}) copy-start(bf16[4356,66]{0,1:T(8,128)(2,1)} %param.8) | copy-start | bytes 1724980
  14.4 0.7 %copy-start.2 = (s32[6,6]{1,0:T(8,128)S(1)}, s32[6,6]{1,0:T(8,128)}, u32[]{:S(2)}) copy-start(s32[6,6]{1,0:T(8,128)} %refs_0_.2) | copy-start | bytes 436
  16.5 0.7 %copy-start = (bf16[80,2304]{1,0:T(8,128)(2,1)}, bf16[80,2304]{1,0:T(8,128)(2,1)S(1)}, u32[]{:S(2)}) copy-start(bf16[80,2304]{1,0:T(8,128)(2,1)S(1)} %shard_map.55.refs_8_) | copy-start | bytes 1105924
  17.9 0.6 %copy-start.6 = (f32[24,1,816]{2,1,0:T(1,128)}, f32[24,1,816]{2,1,0:T(1,128)S(1)}, u32[]{:S(2)}) copy-start(f32[24,1,816]{2,1,0:T(1,128)S(1)} %collective-permute-done.2.refs_4_) | copy-start | bytes 235012
  17.9 0.7 %copy-start.7 = (f32[24,1,816]{2,1,0:T(1,128)}, f32[24,1,816]{2,1,0:T(1,128)S(1)}, u32[]{:S(2)}) copy-start(f32[24,1,816]{2,1,0:T(1,128)S(1)} %collective-permute-done.3.refs_5_) | copy-start | bytes 235012
  17.9 0.7 %copy-start.4 = (f32[48,816]{1,0:T(8,128)}, f32[48,816]{1,0:T(8,128)S(1)}, u32[]{:S(2)}) copy-start(f32[48,816]{1,0:T(8,128)S(1)} %collective-permute-done.refs_2_) | copy-start | bytes 470020
  18.6 0.7 %copy-start.5 = (f32[48,816]{1,0:T(8,128)}, f32[48,816]{1,0:T(8,128)S(1)}, u32[]{:S(2)}) copy-start(f32[48,816]{1,0:T(8,128)S(1)} %collective-permute-done.1.refs_3_) | copy-start | bytes 470020

commit v5 on v4

--- a/solution.py
+++ b/solution.py
@@ -149,9 +149,10 @@
     def upwind(face, before, after):
         return jnp.maximum(face, 0.0) * before + jnp.minimum(face, 0.0) * after
 
+    left = left_ref[...].astype(jnp.float32)
     u_first = w_ref[0][:, :levels]
-    face = spread(0.5 * (left_ref[:, width : width + levels] + u_first))
-    flux_ref[...] = upwind(face, left_ref[:, :width], q_ref[0])
+    face = spread(0.5 * (left[:, width : width + levels] + u_first))
+    flux_ref[...] = upwind(face, left[:, :width], q_ref[0])
 
     def advect(x, q_next, u_next):
         here = q_ref[x]
@@ -182,7 +183,8 @@
         return carry
 
     lax.fori_loop(0, size_x - 1, advect_inner, 0)
-    advect(size_x - 1, right_ref[:, :width], right_ref[:, width : width + levels])
+    right = right_ref[...].astype(jnp.float32)
+    advect(size_x - 1, right[:, :width], right[:, width : width + levels])
 
     runs = pair_blocks(chan)
     per_chunk = DEPTH // ROWS
@@ -251,10 +253,11 @@
     chan = width // levels
     sides = []
     for axis, dim in (("gx", 0), ("gy", 1)):
+        kind = jnp.bfloat16 if dim == 0 else jnp.float32
         last, first, up, down = edges(hydro, axis, dim)
         wlast, wfirst, _, _ = edges(winds, axis, dim)
-        sides.append(lax.ppermute(jnp.concatenate([last, wlast], axis=-1), axis, up))
-        sides.append(lax.ppermute(jnp.concatenate([first, wfirst], axis=-1), axis, down))
+        sides.append(lax.ppermute(jnp.concatenate([last, wlast], axis=-1).astype(kind), axis, up))
+        sides.append(lax.ppermute(jnp.concatenate([first, wfirst], axis=-1).astype(kind), axis, down))
     fold = folded_kernel(coal_kernel, block_mask, chan)
     onto = (jnp.arange(levels)[:, None] == jnp.arange(width)[None, :] // chan).astype(jnp.bfloat16)
     onto = jnp.concatenate([onto] * 3, axis=0)

time: 47.8 us -> 46.6 us (0.975)
  local copies, waits for them, and re-layouts: 8.35 us -> 5.37 us
  other arithmetic: 1.05 us -> 3.48 us
  waiting for transfers between devices: 0.57 us -> 0.01 us
    another operation x0 -> x2, other arithmetic: none -> 2.42 us
    unnamed x17 -> x19, local copies, waits for them, and re-layouts: 4.49 us -> 3.24 us
    squeeze x2, local copies, waits for them, and re-layouts: 1.03 us -> 0.02 us  [edges(): first = lax.index_in_dim(array, 0, dim, keepdims=dim > 0)]
    reshape x1, local copies, waits for them, and re-layouts: 1.38 us -> 0.67 us  [per_device(): mask = cloud_mask.reshape(-1, 1, LANES)]
    ppermute x4, waiting for transfers between devices: 0.57 us -> 0.01 us  [the longest x2 0.01 us: per_device(): lax.ppermute(jnp.concatenate([first, wfirst], axis=-1).astype(kind), axis...]
  transfers between devices with their start and end apart: 4 -> 4, of which waited for: 1 -> 0; matrix products, arithmetic and copies ran while one was open for 7% -> 9% of each run, Pallas kernels for 3% -> 3%
where the time goes in v5:
time: 46.6 us; the launch traced here: 46.4 us
  Pallas kernels  29.5 us (63%)
  starting transfers between devices  7.85 us (17%)
  local copies, waits for them, and re-layouts  5.37 us (12%)
  other arithmetic  3.48 us (7%)
    pallas_call x1, Pallas kernels, per_device(): pl.pallas_call(lambda *refs: step_kernel(levels, chan, *refs), out_shape=...  28.1 us
    ppermute x2, starting transfers between devices, per_device(): lax.ppermute(jnp.concatenate([first, wfirst], axis=-1).astype(kind), axis...  5.08 us
    unnamed x19, local copies, waits for them, and re-layouts  3.24 us
    ppermute x2, starting transfers between devices, per_device(): lax.ppermute(jnp.concatenate([last, wlast], axis=-1).astype(kind), axis, up)  2.76 us
    another operation x2, other arithmetic  2.42 us
    slice x2, local copies, waits for them, and re-layouts, edges(): first = lax.index_in_dim(array, 0, dim, keepdims=dim > 0)  1.45 us
    pallas_call x1, Pallas kernels, folded_kernel(): pl.pallas_call(lambda *refs: fold_kernel(chan, *refs), out_shape=jax.Shap...  1.37 us
  transfers between devices with their start and end apart: 4, of which 0 were waited for; matrix products, arithmetic and copies ran while one was open for 9% of the time, Pallas kernels for 3%

profile of v5, /device:TPU:0, one launch (start us, length us, event | category | flops | bytes accessed | tf_op | source)
XLA Modules:
  0.0 46.4 jit_solution(5172446262838174013)
XLA Ops:
  0.0 1.4 %fusion.3 = (f32[24,1,792]{2,1,0:T(1,128)S(1)}, f32[24,1,792]{2,1,0:T(1,128)S(1)}) fusion(f32[24,48,792]{2,1,0:T(8,128)} %refs_0_.3), kind=kLoop, calls=%fused_computation.17 | loop fusion | bytes 304128 | tf_op jit(solution)/shard_map/slice | solution.py:23
  1.4 1.2 %copy.9.refs_1_ = f32[24,48,24]{2,1,0:T(8,128)S(1)} copy(f32[24,48,24]{1,2,0:T(8,128)} %param.6) | data formatting | bytes 221184 | tf_op args[1]
  2.6 0.0 copy-start.3
  2.6 0.0 copy-start.8
  2.7 0.0 copy-start.1
  2.7 0.0 copy-start.2
  2.7 0.1 pad_maximum_fusion.2
  2.8 0.5 %collective-permute-start.2 = (f32[24,1,816]{2,1,0:T(1,128)S(1)}, f32[24,1,816]{2,1,0:T(1,128)S(1)}, u32[]{:S(2)}, u32[]{:S(2)}) collective-permute-start(f32[24,1,816]{2,1,0:T(1,128)S(1)} %pad_maximum_fusion.2), channel_id=1, source_target_pairs={{0,1},{1,2},{2,3},{3,0},{4,5},{5,6},{6,7},{7,4},{8,9},{9,10},{10,1... | collective-permute-start | bytes 235016 | tf_op jit(solution)/shard_map/ppermute | solution.py:259
  3.3 0.1 pad_maximum_fusion.3
  3.4 2.0 %collective-permute-start.3 = (f32[24,1,816]{2,1,0:T(1,128)S(1)}, f32[24,1,816]{2,1,0:T(1,128)S(1)}, u32[]{:S(2)}, u32[]{:S(2)}) collective-permute-start(f32[24,1,816]{2,1,0:T(1,128)S(1)} %pad_maximum_fusion.3), channel_id=1, source_target_pairs={{1,0},{2,1},{3,2},{0,3},{5,4},{6,5},{7,6},{4,7},{9,8},{10,9},{11,1... | collective-permute-start | bytes 235016 | tf_op jit(solution)/shard_map/ppermute | solution.py:260
  5.5 2.4 %convert.17 = bf16[24,48,792]{2,1,0:T(8,128)(2,1)S(1)} convert(f32[24,48,792]{2,1,0:T(8,128)} %refs_0_.3) | non-fusion elementwise | flops 912384 | bytes 5474304 | tf_op jit(solution)/shard_map/convert.12
  7.9 0.1 pad_maximum_fusion
  8.0 2.3 %collective-permute-start = (bf16[48,816]{1,0:T(8,128)(2,1)S(1)}, bf16[48,816]{1,0:T(8,128)(2,1)S(1)}, u32[]{:S(2)}, u32[]{:S(2)}) collective-permute-start(bf16[48,816]{1,0:T(8,128)(2,1)S(1)} %pad_maximum_fusion), channel_id=1, source_target_pairs={{0,4},{4,8},{8,12},{12,16},{16,20},{20,24},{24,28},{28,0},{1,5},{5... | collective-permute-start | bytes 235016 | tf_op jit(solution)/shard_map/ppermute | solution.py:259
  10.3 0.1 pad_maximum_fusion.1
  10.3 0.0 copy-done.3
  10.4 3.1 %collective-permute-start.1 = (bf16[48,816]{1,0:T(8,128)(2,1)S(1)}, bf16[48,816]{1,0:T(8,128)(2,1)S(1)}, u32[]{:S(2)}, u32[]{:S(2)}) collective-permute-start(bf16[48,816]{1,0:T(8,128)(2,1)S(1)} %pad_maximum_fusion.1), channel_id=1, source_target_pairs={{4,0},{8,4},{12,8},{16,12},{20,16},{24,20},{28,24},{0,28},{5,1},{9... | collective-permute-start | bytes 235016 | tf_op jit(solution)/shard_map/ppermute | solution.py:260
  13.4 0.0 copy-done.8
  13.4 0.7 %reshape.29.refs_6_ = s32[9,1,128]{2,1,0:T(1,128)} reshape(s32[24,48]{1,0:T(8,128)S(1)} %copy-done.8) | data formatting | bytes 9216 | tf_op jit(solution)/shard_map/reshape | solution.py:264
  14.1 0.0 copy-done.1
  14.1 0.0 copy-done.2
  14.1 1.4 %shard_map.55.refs_8_ = bf16[80,2304]{1,0:T(8,128)(2,1)S(1)} custom-call(s32[6,6]{1,0:T(8,128)S(1)} %copy-done.2, bf16[66,4356]{1,0:T(8,128)(2,1)S(1)} %bitcast.10), custom_call_target="tpu_custom_call" | custom-call | flops 33554432 | bytes 4194304 | tf_op jit(solution)/shard_map/pallas_call | solution.py:93
  15.5 0.0 copy-start
  15.5 0.7 %copy-done = bf16[80,2304]{1,0:T(8,128)(2,1)} copy-done((bf16[80,2304]{1,0:T(8,128)(2,1)}, bf16[80,2304]{1,0:T(8,128)(2,1)S(1)}, u32[]{:S(2)}) %copy-start) | copy-done | bytes 368664
  16.2 0.7 %add_convert_fusion.refs_7_ = bf16[36,792]{1,0:T(8,128)(2,1)} fusion(pred[12,792]{1,0:T(8,128)(4,1)S(1)} %iota_compare_fusion), kind=kLoop, calls=%fused_computation | loop fusion | flops 85536 | bytes 66528 | tf_op jit(solution)/shard_map/concatenate | solution.py:263
  16.9 0.0 collective-permute-done.2.refs_4_
  16.9 0.0 copy-start.4
  16.9 0.0 collective-permute-done.3.refs_5_
  16.9 0.0 copy-start.5
  16.9 0.0 collective-permute-done.refs_2_
  16.9 0.0 copy-start.6
  16.9 0.0 collective-permute-done.1.refs_3_
  16.9 0.6 %copy-done.4 = f32[24,1,816]{2,1,0:T(1,128)} copy-done((f32[24,1,816]{2,1,0:T(1,128)}, f32[24,1,816]{2,1,0:T(1,128)S(1)}, u32[]{:S(2)}) %copy-start.4) | copy-done | bytes 78360
  17.5 0.0 copy-done.5
  17.6 0.0 copy-done.6
  17.6 0.0 copy-start.7
  17.6 0.6 %copy-done.7 = bf16[48,816]{1,0:T(8,128)(2,1)} copy-done((bf16[48,816]{1,0:T(8,128)(2,1)}, bf16[48,816]{1,0:T(8,128)(2,1)S(1)}, u32[]{:S(2)}) %copy-start.7) | copy-done | bytes 78360
  18.2 28.1 %shard_map.56 = f32[1152,792]{1,0:T(8,128)} custom-call(f32[24,48,792]{2,1,0:T(8,128)} %refs_0_.3, f32[24,48,24]{2,1,0:T(8,128)} %copy-done.3, bf16[48,816]{1,0:T(8,128)(2,1)} %copy-done.6, bf16[48,816]{1,0:T(8,128)(2,1)} %copy-done.7, f32[24,1,816]{2,1,0:T(1,128)} %copy-done.4, f32[24,1,816]{2,1,0:T(1,128)} %copy-done.5, s32[9,1,128]{2,1,0:T(1,128)} %reshape.29.refs_6_, ...), custom_call_target="tpu_custom_call" | custom-call | tf_op jit(solution)/shard_map/pallas_call | solution.py:266
  (6 shorter events, 0.1 us)
Async XLA Ops:
  2.6 7.7 %copy-start.3 = (f32[24,48,24]{2,1,0:T(8,128)}, f32[24,48,24]{2,1,0:T(8,128)S(1)}, u32[]{:S(2)}) copy-start(f32[24,48,24]{2,1,0:T(8,128)S(1)} %copy.9.refs_1_) | copy-start | bytes 331780
  2.6 10.8 %copy-start.8 = (s32[24,48]{1,0:T(8,128)S(1)}, s32[24,48]{1,0:T(8,128)}, u32[]{:S(2)}) copy-start(s32[24,48]{1,0:T(8,128)} %param.7) | copy-start | bytes 13828
  2.7 11.4 %copy-start.1 = (bf16[4356,66]{0,1:T(8,128)(2,1)S(1)}, bf16[4356,66]{0,1:T(8,128)(2,1)}, u32[]{:S(2)}) copy-start(bf16[4356,66]{0,1:T(8,128)(2,1)} %param.8) | copy-start | bytes 1724980
  2.7 11.4 %copy-start.2 = (s32[6,6]{1,0:T(8,128)S(1)}, s32[6,6]{1,0:T(8,128)}, u32[]{:S(2)}) copy-start(s32[6,6]{1,0:T(8,128)} %refs_0_.2) | copy-start | bytes 436
  2.8 14.1 %collective-permute-start.2 = (f32[24,1,816]{2,1,0:T(1,128)S(1)}, f32[24,1,816]{2,1,0:T(1,128)S(1)}, u32[]{:S(2)}, u32[]{:S(2)}) collective-permute-start(f32[24,1,816]{2,1,0:T(1,128)S(1)} %pad_maximum_fusion.2), channel_id=1, source_target_pairs={{0,1},{1,2},{2,3},{3,0},{4,5},{5,6},{6,7},{7,4},{8,9},{9,10},{10,1... | collective-permute-start | bytes 235016 | tf_op jit(solution)/shard_map/ppermute | solution.py:259
  3.4 13.5 %collective-permute-start.3 = (f32[24,1,816]{2,1,0:T(1,128)S(1)}, f32[24,1,816]{2,1,0:T(1,128)S(1)}, u32[]{:S(2)}, u32[]{:S(2)}) collective-permute-start(f32[24,1,816]{2,1,0:T(1,128)S(1)} %pad_maximum_fusion.3), channel_id=1, source_target_pairs={{1,0},{2,1},{3,2},{0,3},{5,4},{6,5},{7,6},{4,7},{9,8},{10,9},{11,1... | collective-permute-start | bytes 235016 | tf_op jit(solution)/shard_map/ppermute | solution.py:260
  8.0 8.9 %collective-permute-start = (bf16[48,816]{1,0:T(8,128)(2,1)S(1)}, bf16[48,816]{1,0:T(8,128)(2,1)S(1)}, u32[]{:S(2)}, u32[]{:S(2)}) collective-permute-start(bf16[48,816]{1,0:T(8,128)(2,1)S(1)} %pad_maximum_fusion), channel_id=1, source_target_pairs={{0,4},{4,8},{8,12},{12,16},{16,20},{20,24},{24,28},{28,0},{1,5},{5... | collective-permute-start | bytes 235016 | tf_op jit(solution)/shard_map/ppermute | solution.py:259
  10.4 6.6 %collective-permute-start.1 = (bf16[48,816]{1,0:T(8,128)(2,1)S(1)}, bf16[48,816]{1,0:T(8,128)(2,1)S(1)}, u32[]{:S(2)}, u32[]{:S(2)}) collective-permute-start(bf16[48,816]{1,0:T(8,128)(2,1)S(1)} %pad_maximum_fusion.1), channel_id=1, source_target_pairs={{4,0},{8,4},{12,8},{16,12},{20,16},{24,20},{28,24},{0,28},{5,1},{9... | collective-permute-start | bytes 235016 | tf_op jit(solution)/shard_map/ppermute | solution.py:260
  15.5 0.7 %copy-start = (bf16[80,2304]{1,0:T(8,128)(2,1)}, bf16[80,2304]{1,0:T(8,128)(2,1)S(1)}, u32[]{:S(2)}) copy-start(bf16[80,2304]{1,0:T(8,128)(2,1)S(1)} %shard_map.55.refs_8_) | copy-start | bytes 1105924
  16.9 0.6 %copy-start.4 = (f32[24,1,816]{2,1,0:T(1,128)}, f32[24,1,816]{2,1,0:T(1,128)S(1)}, u32[]{:S(2)}) copy-start(f32[24,1,816]{2,1,0:T(1,128)S(1)} %collective-permute-done.2.refs_4_) | copy-start | bytes 235012
  16.9 0.7 %copy-start.5 = (f32[24,1,816]{2,1,0:T(1,128)}, f32[24,1,816]{2,1,0:T(1,128)S(1)}, u32[]{:S(2)}) copy-start(f32[24,1,816]{2,1,0:T(1,128)S(1)} %collective-permute-done.3.refs_5_) | copy-start | bytes 235012
  16.9 0.7 %copy-start.6 = (bf16[48,816]{1,0:T(8,128)(2,1)}, bf16[48,816]{1,0:T(8,128)(2,1)S(1)}, u32[]{:S(2)}) copy-start(bf16[48,816]{1,0:T(8,128)(2,1)S(1)} %collective-permute-done.refs_2_) | copy-start | bytes 235012
  17.6 0.6 %copy-start.7 = (bf16[48,816]{1,0:T(8,128)(2,1)}, bf16[48,816]{1,0:T(8,128)(2,1)S(1)}, u32[]{:S(2)}) copy-start(bf16[48,816]{1,0:T(8,128)(2,1)S(1)} %collective-permute-done.1.refs_3_) | copy-start | bytes 235012
